TPU v7x, 128 devices: a whole 4x4x4 slice. The times are simulated.
128 devices in a mesh: cp: 16 (over x, y), sc: 8 (over z, core).
Axes of the slice: x: 4, y: 4, z: 4, core: 2. Of those that a mesh axis runs over, the one named last changes fastest.
Arguments:
- factors: bfloat16 [32768, 256], P('sc'), may hold values from -6 to 6
- loadings: bfloat16 [65536, 256], P('cp'), may hold values from -0.375 to 0.375
- thresholds: bfloat16 [65536], P('cp'), may hold values from -2.5 to -0.5
- exposures: bfloat16 [65536, 8], P('cp'), may hold values from 0.099609375 to 1
- aversion: float32 [8], replicated, may hold values from 20 to 2000
- lengths: int32 [16], replicated, may hold values from 1 to 4096, 32768 in all
Outputs:
- grad_load: float32 [65536, 256], P('cp', 'sc')
- grad_thresh: float32 [65536], P('cp')
- grad_expo: float32 [65536, 8], P('cp')
- risk: float32 [8], replicated
Inputs may be any that keep to these rules, and one draw needn't show every extreme that they name: `lengths`: each entry counts the live counterparties at the head of its block of 4096 slots; they sum to 32768 and the largest is exactly 4096.
All inputs are finite; a program needn't handle non-finite values.
Results may differ from a plain program's by a relative error of at most 0.0041.
Values may be sent and summed in bfloat16 or wider, within the bound.
A program may use at most 256 MiB of HBM per device.

v0:
```python
import jax
import jax.numpy as jnp
from jax import lax
from jax.sharding import PartitionSpec as P

INV_ROOT_TWO = 0.7071067811865476
INV_ROOT_TWOPI = 0.3989422804014327


def normal_cdf(values):
    return 0.5 * lax.erfc(-values * INV_ROOT_TWO)


def normal_pdf(values):
    return INV_ROOT_TWOPI * jnp.exp(-0.5 * values * values)


def row_scale(load_rows):
    loads32 = load_rows.astype(jnp.float32)
    return jnp.sqrt(1.0 + jnp.sum(loads32 * loads32, axis=1))


def forward_rows(factors, load_rows, limit_rows, expo_rows, live_mask):
    project = lax.dot_general(
        factors, load_rows, (((1,), (1,)), ((), ())), preferred_element_type=jnp.float32
    )
    scaled = row_scale(load_rows)
    latent = (limit_rows.astype(jnp.float32)[None, :] - project) / scaled[None, :]
    probab = (live_mask[None, :] * normal_cdf(latent)).astype(jnp.bfloat16)
    partial_loss = jnp.dot(probab, expo_rows, preferred_element_type=jnp.float32)
    return (latent, probab, partial_loss)


def backward_rows(factors, expo_rows, live_mask, latent, probab, weights, live_total):
    pull_grad = (
        lax.dot_general(
            weights, expo_rows, (((1,), (1,)), ((), ())), preferred_element_type=jnp.float32
        )
        * (live_mask / live_total)[None, :]
    )
    heavy_grad = pull_grad * normal_pdf(latent)
    load_part = lax.dot_general(
        heavy_grad.astype(jnp.bfloat16),
        factors,
        (((0,), (0,)), ((), ())),
        preferred_element_type=jnp.float32,
    )
    lat_part = jnp.sum(heavy_grad * latent, axis=0)
    thr_part = jnp.sum(heavy_grad, axis=0)
    expo_part = (
        lax.dot_general(
            probab, weights, (((0,), (0,)), ((), ())), preferred_element_type=jnp.float32
        )
        / live_total
    )
    return (load_part, lat_part, thr_part, expo_part)


def reduce_scen(load_part, lat_part, thr_part, expo_part):
    load_share = lax.psum_scatter(load_part, "sc", scatter_dimension=1, tiled=True)
    lat_sum, thr_sum, expo_sum = lax.psum((lat_part, thr_part, expo_part), "sc")
    return (load_share, lat_sum, thr_sum, expo_sum)


def finish(load_rows, load_share, lat_sum, thr_sum):
    share_width = load_share.shape[1]
    scaled = row_scale(load_rows)
    column = lax.axis_index("sc") * share_width
    own_cols = lax.dynamic_slice_in_dim(load_rows.astype(jnp.float32), column, share_width, 1)
    grad_load = -load_share / scaled[:, None] - (lat_sum / (scaled * scaled))[:, None] * own_cols
    grad_thresh = thr_sum / scaled
    return (grad_load, grad_thresh)


def scenario_stats(scores):
    top_score = lax.pmax(jnp.max(scores, axis=0), "sc")
    total_mass = lax.psum(jnp.sum(jnp.exp(scores - top_score[None, :]), axis=0), "sc")
    return (top_score, total_mass)


def softmax_part(partial_loss, aversion, scen_total, live_total):
    loss_sum = lax.psum(partial_loss, "cp")
    scores = aversion[None, :] * (loss_sum / live_total)
    top_score, total_mass = scenario_stats(scores)
    weights = (jnp.exp(scores - top_score[None, :]) / total_mass[None, :]).astype(jnp.bfloat16)
    risk = (top_score + jnp.log(total_mass / scen_total)) / aversion
    return (weights, risk)


def per_device(factors, loadings, thresholds, exposures, aversion, lengths):
    cp_count = lax.axis_size("cp")
    sc_count = lax.axis_size("sc")
    position = lax.axis_index("cp")
    row_count = loadings.shape[0]
    factor_width = loadings.shape[1]
    date_count = exposures.shape[1]
    scen_total = float(factors.shape[0] * sc_count)
    live_total = float(row_count * cp_count // 2)
    stride_rows = row_count // cp_count
    received = (
        lax.all_to_all(
            loadings.reshape(stride_rows, cp_count, factor_width),
            "cp",
            split_axis=1,
            concat_axis=1,
            tiled=True,
        ),
        lax.all_to_all(
            thresholds.reshape(stride_rows, cp_count), "cp", split_axis=1, concat_axis=1, tiled=True
        ),
        lax.all_to_all(
            exposures.reshape(stride_rows, cp_count, date_count),
            "cp",
            split_axis=1,
            concat_axis=1,
            tiled=True,
        ),
    )
    loads_in = received[0].reshape(row_count, factor_width)
    limits_in = received[1].reshape(row_count)
    expos_in = received[2].reshape(row_count, date_count)
    source = jnp.arange(cp_count, dtype=jnp.int32)
    counts = jnp.maximum((lengths - position + cp_count - 1) // cp_count, 0)
    end_at = jnp.cumsum(counts)
    starts = end_at - counts
    filled = end_at[-1]
    capacity = row_count // 2 + cp_count
    slot_ids = jnp.arange(capacity, dtype=jnp.int32)
    owner_ids = jnp.sum((slot_ids[:, None] >= end_at[None, :]).astype(jnp.int32), axis=1)
    matches = owner_ids[:, None] == source[None, :]
    start_of = jnp.sum(jnp.where(matches, starts[None, :], 0), axis=1)
    flat_index = (slot_ids - start_of) * cp_count + owner_ids
    alive_slot = slot_ids < filled
    fetch_at = jnp.where(alive_slot, flat_index, 0)
    place_at = jnp.where(alive_slot, flat_index, row_count)
    live_mask = alive_slot.astype(jnp.float32)
    load_rows = loads_in[fetch_at]
    limit_rows = limits_in[fetch_at]
    expo_rows = expos_in[fetch_at]
    latent, probab, partial_loss = forward_rows(
        factors, load_rows, limit_rows, expo_rows, live_mask
    )
    weights, risk = softmax_part(partial_loss, aversion, scen_total, live_total)
    partials = backward_rows(factors, expo_rows, live_mask, latent, probab, weights, live_total)

    def spread(values):
        shape = (row_count,) + values.shape[1:]
        placed = jnp.zeros(shape, values.dtype).at[place_at].set(values, mode="drop")
        return placed.reshape((stride_rows, cp_count) + values.shape[1:])

    returned = (
        lax.all_to_all(spread(partials[0]), "cp", split_axis=1, concat_axis=1, tiled=True),
        lax.all_to_all(spread(partials[1]), "cp", split_axis=1, concat_axis=1, tiled=True),
        lax.all_to_all(spread(partials[2]), "cp", split_axis=1, concat_axis=1, tiled=True),
        lax.all_to_all(spread(partials[3]), "cp", split_axis=1, concat_axis=1, tiled=True),
    )
    load_share, lat_sum, thr_sum, grad_expo = reduce_scen(
        returned[0].reshape(row_count, factor_width),
        returned[1].reshape(row_count),
        returned[2].reshape(row_count),
        returned[3].reshape(row_count, date_count),
    )
    grad_load, grad_thresh = finish(loadings, load_share, lat_sum, thr_sum)
    return (grad_load, grad_thresh, grad_expo, risk)


def solution(mesh):
    in_specs = (P("sc", None), P("cp", None), P("cp"), P("cp", None), P(), P())
    out_specs = (P("cp", "sc"), P("cp"), P("cp", None), P())
    return jax.shard_map(
        per_device, mesh=mesh, in_specs=in_specs, out_specs=out_specs, check_vma=False
    )
```

profile of v0, /device:TPU:0, one launch (start us, length us, event | category | flops | bytes accessed | tf_op | source)
XLA Modules:
  0.0 573.1 jit_solution(5014687287342433227)
XLA Ops:
  10.0 7.1 %all-to-all-start = ((bf16[16,2,128]{2,1,0:T(2,128)(2,1)}), bf16[16,2,128]{2,1,0:T(2,128)(2,1)S(1)}, u32[]{:S(2)}, u32[]{:S(2)}) async-start(bf16[16,2,128]{2,1,0:T(2,128)(2,1)} %reshape.230), calls=%async_computation | async-start | bytes 16384 | tf_op jit(solution)/shard_map/all_to_all | solution.py:108
  19.3 5.4 all-to-all-done
  44.1 12.9 %gather_fusion = bf16[2064]{0:T(1024)(128)(2,1)S(1)} fusion(bf16[4096]{0:T(1024)(128)(2,1)S(1)} %reshape.150, s32[3072]{0:T(1024)S(1)} %pad_clamp_fusion), kind=kCustom, calls=%fused_computation | custom fusion | bytes 16512 | tf_op jit(solution)/shard_map/gather | solution.py:138
  58.0 5.5 gather_fusion.2
  72.0 7.2 %gather_fusion.1 = bf16[2064,256]{1,0:T(8,128)(2,1)S(1)} fusion(bf16[4096,256]{1,0:T(8,128)(2,1)} %bitcast.41, s32[3072]{0:T(1024)S(1)} %pad_clamp_fusion), kind=kCustom, calls=%fused_computation.1 | custom fusion | bytes 2121792 | tf_op jit(solution)/shard_map/gather | solution.py:137
  80.3 88.6 %fusion.2 = (bf16[4096,2064]{0,1:T(8,128)(2,1)S(1)}, f32[2064,4096]{1,0:T(8,128)}) fusion(f32[2064]{0:T(1024)S(1)} %get-tuple-element.32, f32[2064]{0:T(1024)S(1)} %get-tuple-element.33, bf16[2064,256]{1,0:T(8,128)(2,1)S(1)} %gather_fusion.1, bf16[4096,256]{1,0:T(8,128)(2,1)S(1)} %copy-done, f32[2064]{0:T(1024)S(1)} %convert_element_type.33), kind=kOutput, calls=%fused_computation.11 | convolution fusion | flops 4886495232 | bytes 53903552 | tf_op jit(solution)/shard_map/dot_general | solution.py:24
  168.9 5.8 %copy-done.1 = bf16[4096,2064]{0,1:T(8,128)(2,1)} copy-done((bf16[4096,2064]{0,1:T(8,128)(2,1)}, bf16[4096,2064]{0,1:T(8,128)(2,1)S(1)}, u32[]{:S(2)}) %copy-start.1) | copy-done | bytes 16908312
  177.7 81.7 %all-reduce.4.cloned.1.call-done = f32[4096,8]{0,1:T(8,128)} async-done(((f32[4096,8]{0,1:T(8,128)}), f32[4096,8]{0,1:T(8,128)}) %all-reduce.4.cloned.1.call-update) | async-done | bytes 131088 | tf_op jit(solution)/shard_map/psum | solution.py:82
  260.5 13.2 %pmax.7 = f32[8]{0:T(128)S(1)} all-reduce(f32[8]{0:T(128)S(1)} %multiply_reduce_fusion.2), channel_id=1, replica_groups=mesh['cp'=16,'sc'=8] {'sc'}, use_global_device_ids=true, to_apply=%region_6.7 | all-reduce | flops 8 | bytes 64 | tf_op jit(solution)/shard_map/pmax | solution.py:76
  275.6 12.6 %psum.36 = f32[8]{0:T(128)S(1)} all-reduce(f32[8]{0:T(128)S(1)} %fusion.20), channel_id=1, replica_groups=mesh['cp'=16,'sc'=8] {'sc'}, use_global_device_ids=true, to_apply=%region_8.9 | all-reduce | flops 8 | bytes 64 | tf_op jit(solution)/shard_map/psum | solution.py:77
  288.2 23.3 %fusion.31 = (f32[2064]{0:T(1024)S(1)}, f32[2064]{0:T(1024)S(1)}, bf16[4096,2064]{0,1:T(8,128)(2,1)}) fusion(f32[2064,4096]{1,0:T(8,128)} %get-tuple-element.30, f32[2064]{0:T(1024)S(1)} %fusion.21, bf16[2064,8]{1,0:T(8,128)(2,1)} %gather_fusion.2, f32[4096,8]{0,1:T(8,128)} %all-reduce.4.cloned.1.call-done, f32[8]{0:T(128)S(1)} %psum.36, f32[8]{0:T(128)S(1)} %pmax.7, ...), kind=kOutput, calls=%fused_computation.77 | convolution fusion | flops 211480544 | bytes 50913824 | tf_op jit(solution)/shard_map/dot_general | solution.py:36
  311.4 9.5 %fusion.14 = f32[2064,256]{1,0:T(8,128)} fusion(bf16[4096,256]{1,0:T(8,128)(2,1)S(1)} %copy-done, bf16[4096,2064]{0,1:T(8,128)(2,1)} %get-tuple-element.31), kind=kOutput, calls=%fused_computation.33 | convolution fusion | flops 4328521728 | bytes 21118976 | tf_op jit(solution)/shard_map/dot_general | solution.py:42
  320.9 15.7 %scatter_custom_fusion = f32[4096,256]{1,0:T(8,128)} fusion(s32[2064]{0:T(1024)} %get-tuple-element.23, f32[2064,256]{1,0:T(8,128)} %fusion.14, f32[]{:T(128)} %constant.46.clone.1), kind=kCustom, calls=%fused_computation.39 | custom fusion | bytes 4194816 | tf_op jit(solution)/shard_map/scatter | solution.py:148
  336.7 4.6 copy.60
  341.3 55.3 %all_to_all.47 = f32[256,16,256]{2,0,1:T(8,128)S(1)} all-to-all(f32[256,16,256]{2,0,1:T(8,128)S(1)} %copy.60), channel_id=1, replica_groups=mesh['cp'=16,'sc'=8] {'cp'}, dimensions={1} | all-to-all | bytes 8388608 | tf_op jit(solution)/shard_map/all_to_all | solution.py:152
  400.9 5.6 copy.73
  413.0 11.3 %scatter_custom_fusion.1 = f32[4096]{0:T(1024)S(1)} fusion(s32[2064]{0:T(1024)} %get-tuple-element.23, f32[2064]{0:T(1024)S(1)} %get-tuple-element.21, f32[]{:T(128)} %constant.46.clone.1), kind=kCustom, calls=%fused_computation.67 | custom fusion | bytes 16896 | tf_op jit(solution)/shard_map/scatter | solution.py:148
  429.0 8.4 %convolution_multiply_fusion = f32[2064,8]{0,1:T(8,128)S(1)} fusion(bf16[4096,2064]{0,1:T(8,128)(2,1)} %copy-done.1, f32[4096,8]{0,1:T(8,128)S(1)} %copy-done.3, f32[8]{0:T(128)S(1)} %psum.36, f32[8]{0:T(128)S(1)} %pmax.7, f32[8]{0:T(128)S(1)} %broadcast_multiply_fusion), kind=kOutput, calls=%fused_computation.36 | convolution fusion | flops 135413888 | bytes 17105504 | tf_op jit(solution)/shard_map/dot_general | solution.py:51
  437.3 11.3 %scatter_custom_fusion.2 = f32[4096]{0:T(1024)S(1)} fusion(s32[2064]{0:T(1024)} %get-tuple-element.23, f32[2064]{0:T(1024)S(1)} %get-tuple-element.20, f32[]{:T(128)} %constant.46.clone.1), kind=kCustom, calls=%fused_computation.65 | custom fusion | bytes 16896 | tf_op jit(solution)/shard_map/scatter | solution.py:148
  449.4 7.5 %all-to-all-start.5 = ((f32[256,16,1]{0,2,1:T(1,128)}), f32[256,16,1]{0,2,1:T(1,128)S(1)}, u32[]{:S(2)}, u32[]{:S(2)}) async-start(f32[256,16,1]{0,2,1:T(1,128)} %copy.64), calls=%async_computation.5 | async-start | bytes 32768 | tf_op jit(solution)/shard_map/all_to_all | solution.py:154
  457.8 11.2 %scatter_custom_fusion.3 = f32[4096,8]{1,0:T(8,128)} fusion(s32[2064]{0:T(1024)} %get-tuple-element.23, f32[2064,8]{1,0:T(8,128)S(1)} %copy.66, f32[]{:T(128)} %constant.46.clone.1), kind=kCustom, calls=%fused_computation.41 | custom fusion | bytes 131584 | tf_op jit(solution)/shard_map/scatter | solution.py:148
  472.3 7.3 %all-to-all-start.6 = ((f32[256,16,8]{0,2,1:T(8,128)}), f32[256,16,8]{0,2,1:T(8,128)S(1)}, u32[]{:S(2)}, u32[]{:S(2)}) async-start(f32[256,16,8]{0,2,1:T(8,128)} %copy.68), calls=%async_computation.6 | async-start | bytes 262144 | tf_op jit(solution)/shard_map/all_to_all | solution.py:155
  479.9 23.9 %all-reduce = (f32[4096]{0:T(1024)S(1)}, f32[4096]{0:T(1024)S(1)}) all-reduce(f32[4096]{0:T(1024)S(1)} %reshape.157, f32[4096]{0:T(1024)S(1)} %reshape.158), channel_id=1, replica_groups=mesh['cp'=16,'sc'=8] {'sc'}, use_global_device_ids=true, to_apply=%region_14.15 | all-reduce | flops 8192 | bytes 65536 | tf_op jit(solution)/shard_map/psum | solution.py:61
  516.5 48.1 %all-reduce.6.cloned.1.call-done = f32[4096,8]{0,1:T(8,128)} async-done(((f32[4096,8]{0,1:T(8,128)}), f32[4096,8]{0,1:T(8,128)}) %all-reduce.6.cloned.1.call-update) | async-done | bytes 131088 | tf_op jit(solution)/shard_map/psum | solution.py:61
  (76 shorter events, 75.6 us)
Async XLA Ops:
  7.2 73.1 %copy-start = (bf16[4096,256]{1,0:T(8,128)(2,1)S(1)}, bf16[4096,256]{1,0:T(8,128)(2,1)}, u32[]{:S(2)}) copy-start(bf16[4096,256]{1,0:T(8,128)(2,1)} %param.6) | copy-start | bytes 6291460
  10.0 14.6 %all-to-all-start = ((bf16[16,2,128]{2,1,0:T(2,128)(2,1)}), bf16[16,2,128]{2,1,0:T(2,128)(2,1)S(1)}, u32[]{:S(2)}, u32[]{:S(2)}) async-start(bf16[16,2,128]{2,1,0:T(2,128)(2,1)} %reshape.230), calls=%async_computation | async-start | bytes 16384 | tf_op jit(solution)/shard_map/all_to_all | solution.py:108
  24.6 11.1 %all-to-all-start.2 = ((bf16[256,16,8]{0,2,1:T(8,128)(2,1)}), bf16[256,16,8]{0,2,1:T(8,128)(2,1)S(1)}, u32[]{:S(2)}, u32[]{:S(2)}) async-start(bf16[256,16,8]{0,2,1:T(8,128)(2,1)} %copy.58), calls=%async_computation.2 | async-start | bytes 131072 | tf_op jit(solution)/shard_map/all_to_all | solution.py:111
  35.8 32.2 %all-to-all-start.1 = ((bf16[256,16,256]{2,0,1:T(8,128)(2,1)}), bf16[256,16,256]{2,0,1:T(8,128)(2,1)}, u32[]{:S(2)}, u32[]{:S(2)}) async-start(bf16[256,16,256]{2,0,1:T(8,128)(2,1)} %copy.56), calls=%async_computation.1 | async-start | bytes 4194304 | tf_op jit(solution)/shard_map/all_to_all | solution.py:101
  40.2 219.2 %all-reduce.4.cloned.1.call-start = ((), (), s32[]{:S(2)}) async-start(), calls=%async_computation.8 | async-start | bytes 262144 | tf_op jit(solution)/shard_map/psum | solution.py:82
  80.3 94.4 %copy-start.2 = (bf16[2064,8]{1,0:T(8,128)(2,1)S(1)}, bf16[2064,8]{1,0:T(8,128)(2,1)}, u32[]{:S(2)}) copy-start(bf16[2064,8]{1,0:T(8,128)(2,1)} %gather_fusion.2) | copy-start | bytes 99076
  80.3 97.5 %copy-start.4 = (f32[8]{0:T(128)S(1)}, f32[8]{0:T(128)}, u32[]{:S(2)}) copy-start(f32[8]{0:T(128)} %param.10) | copy-start | bytes 100
  168.9 5.8 %copy-start.1 = (bf16[4096,2064]{0,1:T(8,128)(2,1)}, bf16[4096,2064]{0,1:T(8,128)(2,1)S(1)}, u32[]{:S(2)}) copy-start(bf16[4096,2064]{0,1:T(8,128)(2,1)S(1)} %get-tuple-element.29) | copy-start | bytes 50724868
  177.7 328.5 %reduce-scatter.4.cloned.1.call-start = ((), (), s32[]{:S(2)}) async-start(), calls=%async_computation.10 | async-start | bytes 4718592
  320.9 108.0 %copy-start.3 = (f32[4096,8]{0,1:T(8,128)S(1)}, f32[4096,8]{0,1:T(8,128)}, u32[]{:S(2)}) copy-start(f32[4096,8]{0,1:T(8,128)} %all-reduce.4.cloned.1.call-done) | copy-start | bytes 393220
  425.1 24.3 %all-to-all-start.4 = ((f32[256,16,1]{0,2,1:T(1,128)}), f32[256,16,1]{0,2,1:T(1,128)S(1)}, u32[]{:S(2)}, u32[]{:S(2)}) async-start(f32[256,16,1]{0,2,1:T(1,128)} %copy.62), calls=%async_computation.4 | async-start | bytes 32768 | tf_op jit(solution)/shard_map/all_to_all | solution.py:153
  449.4 22.9 %all-to-all-start.5 = ((f32[256,16,1]{0,2,1:T(1,128)}), f32[256,16,1]{0,2,1:T(1,128)S(1)}, u32[]{:S(2)}, u32[]{:S(2)}) async-start(f32[256,16,1]{0,2,1:T(1,128)} %copy.64), calls=%async_computation.5 | async-start | bytes 32768 | tf_op jit(solution)/shard_map/all_to_all | solution.py:154
  472.3 32.1 %all-to-all-start.6 = ((f32[256,16,8]{0,2,1:T(8,128)}), f32[256,16,8]{0,2,1:T(8,128)S(1)}, u32[]{:S(2)}, u32[]{:S(2)}) async-start(f32[256,16,8]{0,2,1:T(8,128)} %copy.68), calls=%async_computation.6 | async-start | bytes 262144 | tf_op jit(solution)/shard_map/all_to_all | solution.py:155
  479.7 84.9 %all-reduce.6.cloned.1.call-start = ((), (), s32[]{:S(2)}) async-start(), calls=%async_computation.9 | async-start | bytes 262144 | tf_op jit(solution)/shard_map/psum | solution.py:61
Sparse Core Ops, SparseCore 0:
  177.8 81.5 all-reduce.3
  406.7 34.3 reduce-scatter.3
  506.3 58.2 all-reduce.5
where the time goes:
time: 582 us; the launch traced here: 573 us
  waiting for transfers between devices  144 us (25%)
  matrix products  133 us (23%)
  local copies, waits for them, and re-layouts  124 us (21%)
  blocking collectives  105 us (18%)
  starting transfers between devices  33.8 us (6%)
  other arithmetic  19.5 us (3%)
  between operations  14.5 us (2%)
    dot_general x1, matrix products, forward_rows(): lax.dot_general(factors, load_rows, (((1,), (1,)), ((), ())), preferred_e...  88.6 us
    psum x1, waiting for transfers between devices, softmax_part(): loss_sum = lax.psum(partial_loss, 'cp')  81.7 us
    all_to_all x1, blocking collectives, per_device(): lax.all_to_all(spread(partials[0]), 'cp', split_axis=1, concat_axis=1, ti...  55.3 us
    scatter x4, local copies, waits for them, and re-layouts, spread(): jnp.zeros(shape, values.dtype).at[place_at].set(values, mode='drop')  49.5 us
    psum x1, waiting for transfers between devices, reduce_scen(): lat_sum, thr_sum, expo_sum = lax.psum((lat_part, thr_part, expo_part), 'sc')  48.1 us
    psum x1, blocking collectives, reduce_scen(): lat_sum, thr_sum, expo_sum = lax.psum((lat_part, thr_part, expo_part), 'sc')  23.9 us
    dot_general x1, matrix products, backward_rows(): lax.dot_general(weights, expo_rows, (((1,), (1,)), ((), ())), preferred_e...  23.3 us
    unnamed x17, local copies, waits for them, and re-layouts  20.1 us
  transfers between devices with their start and end apart: 9, of which 5 were waited for; matrix products, arithmetic and copies ran while one was open for 17% of the time, Pallas kernels for 0%

commit v1 on v0

v1 whole, which is shorter than its diff:
```python
import functools
import math

import jax
import jax.numpy as jnp
from jax import lax
from jax.experimental import pallas as pl
from jax.experimental.pallas import tpu as pltpu
from jax.sharding import PartitionSpec as P

MESH = pl.DeviceIdType.MESH
NCP = 16
NSC = 8
F = 256
ROWS = 4096
S = 4096
CAP = 2176
SEG = ROWS // NCP
LIVE = 32768
SCEN = 32768
ST = 512
CHUNK = 544
ROOT_HALF = 0.7071067811865476
LOG2E = 1.4426950408889634
FAR = -3.1
TAIL = (-0.750217616, 0.756257034, -1.37553279, 0.0025935648)
BF = jnp.bfloat16
F32 = jnp.float32


def spots(lengths_ref, position):
    start = jnp.int32(0)
    out = []
    for block in range(NCP):
        live = lengths_ref[block]
        tiles = (live + 15) // 16
        offset = (position - block + NCP) % NCP
        out.append((start, offset, live))
        start = start + (tiles - offset + 15) // 16
    return out


def exchange_kernel(tiles, small, got, got_small, sends, recvs, sends_s, recvs_s, sends_b, recvs_b, own):
    me = lax.axis_index("cp")
    sc = lax.axis_index("sc")
    core = sc % 2
    sibling = sc + 1 - 2 * core
    barrier = pltpu.get_barrier_semaphore()

    def greet(k, _):
        pl.semaphore_signal(barrier, inc=1, device_id=((me + k) % NCP, sc), device_id_type=MESH)
        return 0

    lax.fori_loop(1, NCP, greet, 0)
    pl.semaphore_signal(barrier, inc=1, device_id=(me, sibling), device_id_type=MESH)
    pl.semaphore_wait(barrier, NCP)

    half = pl.ds(core * 8, 8)

    def row_copy(k):
        peer = (me + k) % NCP
        return pltpu.make_async_remote_copy(
            src_ref=tiles.at[half, (peer - me + NCP) % NCP],
            dst_ref=got.at[me, half],
            send_sem=sends.at[k],
            recv_sem=recvs.at[k],
            device_id=(peer, sc),
            device_id_type=MESH,
        )

    def small_copy(k):
        peer = (me + k) % NCP
        return pltpu.make_async_remote_copy(
            src_ref=small.at[(peer - me + NCP) % NCP],
            dst_ref=got_small.at[me],
            send_sem=sends_s.at[k],
            recv_sem=recvs_s.at[k],
            device_id=(peer, sc),
            device_id_type=MESH,
        )

    def forward(k):
        source = (me - k + NCP) % NCP
        return pltpu.make_async_remote_copy(
            src_ref=got.at[source, half],
            dst_ref=got.at[source, half],
            send_sem=sends_b.at[k],
            recv_sem=recvs_b.at[k],
            device_id=(me, sibling),
            device_id_type=MESH,
        )

    def start(k, _):
        row_copy(k).start()
        small_copy(k).start()
        return 0

    lax.fori_loop(1, NCP, start, 0)
    mine = pltpu.make_async_copy(tiles.at[:, 0], got.at[me], own.at[0])
    mine.start()
    mine_small = pltpu.make_async_copy(small.at[0], got_small.at[me], own.at[1])
    mine_small.start()

    def pass_on(k, _):
        row_copy(k).wait_recv()
        forward(k).start()
        return 0

    lax.fori_loop(1, NCP, pass_on, 0)
    mine.wait()
    mine_small.wait()

    def finish(k, _):
        row_copy(k).wait_send()
        small_copy(k).wait()
        forward(k).wait()
        return 0

    lax.fori_loop(1, NCP, finish, 0)


def exchange(tiles, small):
    any_spec = pl.BlockSpec(memory_space=pl.ANY)
    return pl.pallas_call(
        exchange_kernel,
        out_shape=(
            jax.ShapeDtypeStruct((NCP, 16, 16, F), BF),
            jax.ShapeDtypeStruct((NCP, 16, SEG), BF),
        ),
        in_specs=[any_spec] * 2,
        out_specs=[any_spec] * 2,
        scratch_shapes=[pltpu.SemaphoreType.DMA((NCP,))] * 6 + [pltpu.SemaphoreType.DMA((2,))],
        compiler_params=pltpu.CompilerParams(collective_id=0, has_side_effects=True),
        name="exchange",
    )(tiles, small)


def double_cdf(u):
    far = TAIL[3]
    for coef in TAIL[2::-1]:
        far = far * u + coef
    return jnp.where(u < FAR, jnp.exp2(far), 1.0 + lax.erf(u))


def forward_kernel(lengths, got, got_small, factors, prob, loss, comp, shift, slope, expo, wide, expo_t):
    position = lax.axis_index("cp")

    @pl.when(pl.program_id(0) == 0)
    def _():
        comp[...] = jnp.zeros_like(comp)
        wide[...] = jnp.zeros_like(wide)
        index = lax.broadcasted_iota(jnp.int32, (SEG, 128), 0)
        lane = lax.broadcasted_iota(jnp.int32, (SEG, 128), 1)
        for block, (start, offset, live) in enumerate(spots(lengths, position)):
            at = pl.ds(pl.multiple_of(start * 16, 16), SEG)
            comp[at, :] = got[block]
            part = got_small[block].astype(F32)
            part = jnp.concatenate([part, jnp.zeros((112, SEG), F32)], axis=0).T
            row = (offset + 16 * (index // 16)) * 16 + index % 16
            keep = (row < live) | (lane >= 8)
            wide[at, :] = jnp.where(keep, part, 0.0)

        def scale(i, _):
            at = pl.ds(pl.multiple_of(i * 128, 128), 128)
            rows = comp[at, :].astype(F32)
            total = jnp.sum(rows * rows, axis=1, keepdims=True)
            by = lax.rsqrt(1.0 + total) * ROOT_HALF
            slope[at, :] = jnp.broadcast_to(by, (128, 128))
            part = wide[at, :]
            shift[at, :] = jnp.broadcast_to(part[:, 8:9] * by, (128, 128))
            expo[at, :] = part.astype(BF)
            expo_t[:, at] = part.T[0:16, :].astype(BF)
            return 0

        lax.fori_loop(0, CAP // 128, scale, 0)

    def chunk(i, _):
        at = pl.ds(pl.multiple_of(i * CHUNK, 16), CHUNK)
        project = lax.dot_general(
            comp[at, :], factors[...], (((1,), (1,)), ((), ())), preferred_element_type=F32
        )
        a = jnp.concatenate([shift[at, :]] * (ST // 128), axis=1)
        b = jnp.concatenate([slope[at, :]] * (ST // 128), axis=1)
        prob[at, :] = double_cdf(a - project * b).astype(BF)
        return 0

    lax.fori_loop(0, CAP // CHUNK, chunk, 0)
    loss[...] = jnp.dot(expo_t[...], prob[...], preferred_element_type=F32)[0:8, :]


def forward(lengths, got, got_small, factors):
    whole = lambda shape: pl.BlockSpec(shape, lambda i: (0,) * len(shape))
    return pl.pallas_call(
        forward_kernel,
        grid=(S // ST,),
        out_shape=(
            jax.ShapeDtypeStruct((CAP, S), BF),
            jax.ShapeDtypeStruct((8, S), F32),
            jax.ShapeDtypeStruct((CAP + SEG, F), BF),
            jax.ShapeDtypeStruct((CAP, 128), F32),
            jax.ShapeDtypeStruct((CAP, 128), F32),
            jax.ShapeDtypeStruct((CAP, 128), BF),
        ),
        in_specs=[
            pl.BlockSpec(memory_space=pltpu.SMEM),
            whole((NCP, SEG, F)),
            whole((NCP, 16, SEG)),
            pl.BlockSpec((ST, F), lambda i: (i, 0)),
        ],
        out_specs=[
            pl.BlockSpec((CAP, ST), lambda i: (0, i)),
            pl.BlockSpec((8, ST), lambda i: (0, i)),
            whole((CAP + SEG, F)),
            whole((CAP, 128)),
            whole((CAP, 128)),
            whole((CAP, 128)),
        ],
        scratch_shapes=[pltpu.VMEM((CAP + SEG, 128), F32), pltpu.VMEM((16, CAP), BF)],
        compiler_params=pltpu.CompilerParams(vmem_limit_bytes=48 * 2**20),
        name="forward",
    )(lengths, got, got_small, factors)


def softmax_kernel(loss, aversion, weights, risk, parts, mine, every, stats, sends, recvs, sends_g, recvs_g, sends_z, recvs_z):
    me = lax.axis_index("cp")
    sc = lax.axis_index("sc")
    width = S // NCP
    barrier = pltpu.get_barrier_semaphore()

    def greet(k, _):
        pl.semaphore_signal(barrier, inc=1, device_id=((me + k) % NCP, sc), device_id_type=MESH)
        return 0

    def greet_z(k, _):
        pl.semaphore_signal(barrier, inc=1, device_id=(me, (sc + k) % NSC), device_id_type=MESH)
        return 0

    lax.fori_loop(1, NCP, greet, 0)
    lax.fori_loop(1, NSC, greet_z, 0)
    pl.semaphore_wait(barrier, NCP + NSC - 2)

    def part_of(position):
        return pl.ds(pl.multiple_of(position * width, width), width)

    def scatter(k):
        peer = (me + k) % NCP
        return pltpu.make_async_remote_copy(
            src_ref=loss.at[:, part_of(peer)],
            dst_ref=parts.at[me],
            send_sem=sends.at[k],
            recv_sem=recvs.at[k],
            device_id=(peer, sc),
            device_id_type=MESH,
        )

    def gather(k):
        return pltpu.make_async_remote_copy(
            src_ref=mine,
            dst_ref=every.at[:, part_of(me)],
            send_sem=sends_g.at[k],
            recv_sem=recvs_g.at[k],
            device_id=((me + k) % NCP, sc),
            device_id_type=MESH,
        )

    def share(k):
        return pltpu.make_async_remote_copy(
            src_ref=stats.at[sc],
            dst_ref=stats.at[sc],
            send_sem=sends_z.at[k],
            recv_sem=recvs_z.at[k],
            device_id=(me, (sc + k) % NSC),
            device_id_type=MESH,
        )

    def run(count, act):
        def body(k, _):
            act(k)
            return 0

        lax.fori_loop(1, count, body, 0)

    run(NCP, lambda k: scatter(k).start())
    parts[me] = loss[:, part_of(me)]
    run(NCP, lambda k: scatter(k).wait_recv())
    total = parts[0]
    for i in range(1, NCP):
        total = total + parts[i]
    averse = aversion[...]
    averse_two = jnp.concatenate([averse] * (width // 128), axis=1)
    score = averse_two * (total * (0.5 / LIVE))
    mine[...] = score
    run(NCP, lambda k: gather(k).start())
    every[:, part_of(me)] = score
    run(NCP, lambda k: gather(k).wait_recv())
    scores = every[...]
    top = jnp.max(scores, axis=1, keepdims=True)
    raised = jnp.exp(scores - top)
    mass = jnp.sum(raised, axis=1, keepdims=True)
    stats[sc, 0:8, :] = jnp.broadcast_to(top, (8, 128))
    stats[sc, 8:16, :] = jnp.broadcast_to(mass, (8, 128))
    run(NSC, lambda k: share(k).start())
    run(NSC, lambda k: share(k).wait_recv())
    best = stats[0, 0:8, :]
    for i in range(1, NSC):
        best = jnp.maximum(best, stats[i, 0:8, :])
    heap = jnp.zeros((8, 128), F32)
    for i in range(NSC):
        heap = heap + stats[i, 8:16, :] * jnp.exp(stats[i, 0:8, :] - best)
    final = (jnp.exp(scores - best[:, 0:1]) / heap[:, 0:1]).astype(BF)
    weights[...] = jnp.concatenate([final.astype(F32), jnp.zeros((8, S), F32)], axis=0).astype(BF)
    risk[...] = (best + jnp.log(heap / SCEN)) / averse
    run(NCP, lambda k: scatter(k).wait_send())
    run(NCP, lambda k: gather(k).wait_send())
    run(NSC, lambda k: share(k).wait_send())


def softmax(loss, aversion):
    vmem = pl.BlockSpec(memory_space=pltpu.VMEM)
    dma = pltpu.SemaphoreType.DMA
    return pl.pallas_call(
        softmax_kernel,
        out_shape=(jax.ShapeDtypeStruct((16, S), BF), jax.ShapeDtypeStruct((8, 128), F32)),
        in_specs=[vmem] * 2,
        out_specs=[vmem] * 2,
        scratch_shapes=[
            pltpu.VMEM((NCP, 8, S // NCP), F32),
            pltpu.VMEM((8, S // NCP), F32),
            pltpu.VMEM((8, S), F32),
            pltpu.VMEM((NSC, 16, 128), F32),
            dma((NCP,)),
            dma((NCP,)),
            dma((NCP,)),
            dma((NCP,)),
            dma((NSC,)),
            dma((NSC,)),
        ],
        compiler_params=pltpu.CompilerParams(collective_id=1, has_side_effects=True),
        name="softmax",
    )(loss, aversion)


def backward_kernel(comp, shift, slope, expo, factors, weights, prob, out, load_acc, lat_acc, thr_acc, expo_acc, turned):
    step = pl.program_id(0)

    @pl.when(step == 0)
    def _():
        load_acc[...] = jnp.zeros_like(load_acc)
        lat_acc[...] = jnp.zeros_like(lat_acc)
        thr_acc[...] = jnp.zeros_like(thr_acc)
        expo_acc[...] = jnp.zeros_like(expo_acc)

    turned[:, 0:16] = weights[...].astype(F32).T.astype(BF)

    def chunk(i, _):
        at = pl.ds(pl.multiple_of(i * CHUNK, 16), CHUNK)
        project = lax.dot_general(
            comp[at, :], factors[...], (((1,), (1,)), ((), ())), preferred_element_type=F32
        )
        pull = jnp.dot(expo[at, 0:16], weights[...], preferred_element_type=F32)
        a = jnp.concatenate([shift[at, :]] * (ST // 128), axis=1)
        b = jnp.concatenate([slope[at, :]] * (ST // 128), axis=1)
        u = a - project * b
        heavy = pull * jnp.exp2(u * u * (-LOG2E))
        lat = heavy * u
        lat_sum = lat[:, 0:128]
        thr_sum = heavy[:, 0:128]
        for k in range(1, ST // 128):
            lat_sum = lat_sum + lat[:, k * 128 : (k + 1) * 128]
            thr_sum = thr_sum + heavy[:, k * 128 : (k + 1) * 128]
        lat_acc[at, :] += lat_sum
        thr_acc[at, :] += thr_sum
        load_acc[at, :] += jnp.dot(heavy.astype(BF), factors[...], preferred_element_type=F32)
        expo_acc[at, :] += jnp.dot(prob[at, :], turned[:, 0:16], preferred_element_type=F32)
        return 0

    lax.fori_loop(0, CAP // CHUNK, chunk, 0)

    @pl.when(step == pl.num_programs(0) - 1)
    def _():
        scale = 1.0 / (LIVE * math.sqrt(2.0 * math.pi))

        def fold(i, _):
            at = pl.ds(pl.multiple_of(i * 128, 128), 128)
            by = slope[at, 0:1] * math.sqrt(2.0)
            lat = jnp.sum(lat_acc[at, :], axis=1, keepdims=True) * (scale * math.sqrt(2.0))
            thr = jnp.sum(thr_acc[at, :], axis=1, keepdims=True) * scale * by
            rows = comp[at, :].astype(F32)
            grad = -(load_acc[at, :] * (scale * by)) - (lat * by * by) * rows
            flat = grad.T
            dates = jnp.concatenate([expo_acc[at, :], jnp.zeros((128, 112), F32)], axis=1).T
            dates = dates[0:8, :] * (0.5 / LIVE)
            limits = jnp.broadcast_to(thr, (128, 128)).T
            for j in range(NSC):
                out[j, 0:32, at] = flat[32 * j : 32 * (j + 1), :]
                out[j, 32:40, at] = jnp.concatenate(
                    [dates[j : j + 1, :], limits[0:7, :]], axis=0
                )
            return 0

        lax.fori_loop(0, CAP // 128, fold, 0)


def backward(comp, shift, slope, expo, factors, weights, prob):
    whole = lambda shape: pl.BlockSpec(shape, lambda i: (0,) * len(shape))
    return pl.pallas_call(
        backward_kernel,
        grid=(S // ST,),
        out_shape=jax.ShapeDtypeStruct((NSC, 40, CAP), F32),
        in_specs=[
            whole((CAP + SEG, F)),
            whole((CAP, 128)),
            whole((CAP, 128)),
            whole((CAP, 128)),
            pl.BlockSpec((ST, F), lambda i: (i, 0)),
            pl.BlockSpec((16, ST), lambda i: (0, i)),
            pl.BlockSpec((CAP, ST), lambda i: (0, i)),
        ],
        out_specs=whole((NSC, 40, CAP)),
        scratch_shapes=[
            pltpu.VMEM((CAP, F), F32),
            pltpu.VMEM((CAP, 128), F32),
            pltpu.VMEM((CAP, 128), F32),
            pltpu.VMEM((CAP, 16), F32),
            pltpu.VMEM((ST, 128), BF),
        ],
        compiler_params=pltpu.CompilerParams(vmem_limit_bytes=48 * 2**20),
        name="backward",
    )(comp, shift, slope, expo, factors, weights, prob)


def run(first, last, act):
    def body(k, _):
        act(k)
        return 0

    lax.fori_loop(first, last, body, 0)


def add_kernel(grads, full, pair, sum_l, sum_s, near_l, near_s, sends_a, recvs_a, sends_b, recvs_b):
    me = lax.axis_index("cp")
    sc = lax.axis_index("sc")
    core = sc % 2
    z = sc // 2
    sibling = sc + 1 - 2 * core
    barrier = pltpu.get_barrier_semaphore()
    pl.semaphore_signal(barrier, inc=1, device_id=(me, sibling), device_id_type=MESH)
    run(1, 4, lambda k: pl.semaphore_signal(barrier, inc=1, device_id=(me, ((z + k) % 4) * 2 + core), device_id_type=MESH))
    pl.semaphore_wait(barrier, 4)

    def pair_copy(k):
        to = (z + k) % 4
        return pltpu.make_async_remote_copy(
            src_ref=grads.at[to * 2 + 1 - core],
            dst_ref=pair.at[k],
            send_sem=sends_a.at[k],
            recv_sem=recvs_a.at[k],
            device_id=(me, sibling),
            device_id_type=MESH,
        )

    def near_copy(k, which):
        src, dst = ((sum_l, near_l), (sum_s, near_s))[which]
        return pltpu.make_async_remote_copy(
            src_ref=src.at[k],
            dst_ref=dst.at[k],
            send_sem=sends_b.at[which, k],
            recv_sem=recvs_b.at[which, k],
            device_id=(me, ((z + k) % 4) * 2 + core),
            device_id_type=MESH,
        )

    for k in (2, 1, 3, 0):
        pair_copy(k).start()
    for k in (2, 1, 3):
        pair_copy(k).wait_recv()
        share = ((z + k) % 4) * 2 + core
        sum_l[k] = (grads[share, 0:32, :] + pair[k, 0:32, :]).astype(BF)
        sum_s[k] = grads[share, 32:40, :] + pair[k, 32:40, :]
        near_copy(k, 0).start()
        near_copy(k, 1).start()
    pair_copy(0).wait_recv()
    full[:, 0:CAP] = grads[sc] + pair[0]
    for k in (1, 3, 2):
        near_copy(k, 0).wait_recv()
        near_copy(k, 1).wait_recv()
        full[0:32, 0:CAP] += near_l[k].astype(F32)
        full[32:40, 0:CAP] += near_s[k]
    full[:, CAP:] = jnp.zeros((40, 384), F32)
    for k in (0, 1, 2, 3):
        pair_copy(k).wait_send()
        if k:
            near_copy(k, 0).wait_send()
            near_copy(k, 1).wait_send()


def add_up(grads):
    vmem = pl.BlockSpec(memory_space=pltpu.VMEM)
    dma = pltpu.SemaphoreType.DMA
    return pl.pallas_call(
        add_kernel,
        out_shape=jax.ShapeDtypeStruct((40, CAP + 384), F32),
        in_specs=[vmem],
        out_specs=vmem,
        scratch_shapes=[
            pltpu.VMEM((4, 40, CAP), F32),
            pltpu.VMEM((4, 32, CAP), BF),
            pltpu.VMEM((4, 8, CAP), F32),
            pltpu.VMEM((4, 32, CAP), BF),
            pltpu.VMEM((4, 8, CAP), F32),
            dma((4,)),
            dma((4,)),
            dma((2, 4)),
            dma((2, 4)),
        ],
        compiler_params=pltpu.CompilerParams(
            collective_id=2, has_side_effects=True, vmem_limit_bytes=32 * 2**20
        ),
        name="add_up",
    )(grads)


def place_kernel(lengths, full, pack_l, pack_s):
    lane = lax.broadcasted_iota(jnp.int32, (40, SEG), 1)
    for block, (start, offset, live) in enumerate(spots(lengths, lax.axis_index("cp"))):
        at = pl.ds(pl.multiple_of((start // 8) * 128, 128), 384)
        piece = pltpu.roll(full[:, at], (24 - start % 8) * 16 % 384, 1)[:, 0:SEG]
        row = (offset + 16 * (lane // 16)) * 16 + lane % 16
        piece = jnp.where(row < live, piece, 0.0)
        pack_l[block] = piece[0:32, :].astype(BF)
        pack_s[block] = piece[32:40, :]


def place(lengths, full):
    vmem = pl.BlockSpec(memory_space=pltpu.VMEM)
    return pl.pallas_call(
        place_kernel,
        out_shape=(
            jax.ShapeDtypeStruct((NCP, 32, SEG), BF),
            jax.ShapeDtypeStruct((NCP, 8, SEG), F32),
        ),
        in_specs=[pl.BlockSpec(memory_space=pltpu.SMEM), vmem],
        out_specs=[vmem] * 2,
        name="place",
    )(lengths, full)


def return_kernel(
    pack_l, pack_s, load_out, thr_out, expo_out,
    back_l, back_s, line, sends_c, recvs_c, sends_d, recvs_d,
):
    me = lax.axis_index("cp")
    sc = lax.axis_index("sc")
    barrier = pltpu.get_barrier_semaphore()
    run(1, NCP, lambda k: pl.semaphore_signal(barrier, inc=1, device_id=((me + k) % NCP, sc), device_id_type=MESH))
    run(1, NSC, lambda k: pl.semaphore_signal(barrier, inc=1, device_id=(me, (sc + k) % NSC), device_id_type=MESH))
    pl.semaphore_wait(barrier, NCP + NSC - 2)

    def back_copy(k, which):
        src, dst = ((pack_l, back_l), (pack_s, back_s))[which]
        peer = (me + k) % NCP
        return pltpu.make_async_remote_copy(
            src_ref=src.at[peer],
            dst_ref=dst.at[(me - peer + NCP) % NCP],
            send_sem=sends_c.at[which, k],
            recv_sem=recvs_c.at[which, k],
            device_id=(peer, sc),
            device_id_type=MESH,
        )

    run(1, NCP, lambda k: (back_copy(k, 0).start(), back_copy(k, 1).start()))
    back_l[0] = pack_l[me]
    back_s[0] = pack_s[me]
    run(1, NCP, lambda k: (back_copy(k, 0).wait_recv(), back_copy(k, 1).wait_recv()))

    group = lax.broadcasted_iota(jnp.int32, (40, 128), 1) // 16
    for g in range(2):
        for h in range(2):
            held = [
                jnp.concatenate(
                    [
                        back_l[8 * g + q, :, 128 * h : 128 * (h + 1)].astype(F32),
                        back_s[8 * g + q, :, 128 * h : 128 * (h + 1)],
                    ],
                    axis=0,
                )
                for q in range(8)
            ]
            for s in range(8):
                mixed = held[s]
                for q in range(8):
                    if q != s:
                        mixed = jnp.where(group == q, pltpu.roll(held[q], (16 * (q - s)) % 128, 1), mixed)
                    elif s > 0:
                        pass
                tile = 2 * (8 * h + s) + g
                load_out[:, 128 * tile : 128 * (tile + 1)] = mixed[0:32, :]
                line[0:1, 128 * tile : 128 * (tile + 1)] = mixed[32:33, :]
                thr_out[:, 128 * tile : 128 * (tile + 1)] = mixed[33:34, :]

    expo_out[sc] = line[...]

    def date_copy(k):
        return pltpu.make_async_remote_copy(
            src_ref=line,
            dst_ref=expo_out.at[sc],
            send_sem=sends_d.at[k],
            recv_sem=recvs_d.at[k],
            device_id=(me, (sc + k) % NSC),
            device_id_type=MESH,
        )

    run(1, NSC, lambda k: date_copy(k).start())
    run(1, NSC, lambda k: date_copy(k).wait())
    run(1, NCP, lambda k: (back_copy(k, 0).wait_send(), back_copy(k, 1).wait_send()))


def give_back(pack_l, pack_s):
    vmem = pl.BlockSpec(memory_space=pltpu.VMEM)
    dma = pltpu.SemaphoreType.DMA
    return pl.pallas_call(
        return_kernel,
        out_shape=(
            jax.ShapeDtypeStruct((32, ROWS), F32),
            jax.ShapeDtypeStruct((1, ROWS), F32),
            jax.ShapeDtypeStruct((NSC, 1, ROWS), F32),
        ),
        in_specs=[vmem] * 2,
        out_specs=[vmem] * 3,
        scratch_shapes=[
            pltpu.VMEM((NCP, 32, SEG), BF),
            pltpu.VMEM((NCP, 8, SEG), F32),
            pltpu.VMEM((1, ROWS), F32),
            dma((2, NCP)),
            dma((2, NCP)),
            dma((NSC,)),
            dma((NSC,)),
        ],
        compiler_params=pltpu.CompilerParams(collective_id=3, has_side_effects=True),
        name="give_back",
    )(pack_l, pack_s)


def per_device(factors, loadings, thresholds, exposures, aversion, lengths):
    tiles = loadings.reshape(16, NCP, 16, F)
    small = jnp.concatenate(
        [exposures.T, thresholds[None, :], jnp.zeros((7, ROWS), BF)], axis=0
    )
    small = small.reshape(16, 16, NCP, 16).transpose(2, 0, 1, 3).reshape(NCP, 16, SEG)
    got, got_small = exchange(tiles, small)
    prob, loss, comp, shift, slope, expo = forward(
        lengths, got.reshape(NCP, SEG, F), got_small, factors
    )
    weights, risk = softmax(loss, jnp.broadcast_to(aversion[:, None], (8, 128)))
    grads = backward(comp, shift, slope, expo, factors, weights, prob)
    load, thr, dates = give_back(*place(lengths, add_up(grads)))
    return (load.T, thr.reshape(ROWS), dates.reshape(NSC, ROWS).T, risk[:, 0])


def solution(mesh):
    in_specs = (P("sc", None), P("cp", None), P("cp"), P("cp", None), P(), P())
    out_specs = (P("cp", "sc"), P("cp"), P("cp", None), P())
    return jax.shard_map(
        per_device, mesh=mesh, in_specs=in_specs, out_specs=out_specs, check_vma=False
    )
```

time: 582 us -> 174 us (0.30); the launches traced: 573 us -> 172 us
  Pallas kernels: 0 us -> 154 us
  waiting for transfers between devices: 144 us -> 0 us
  matrix products: 133 us -> 0 us
  local copies, waits for them, and re-layouts: 124 us -> 17.6 us
  blocking collectives: 105 us -> 0 us
  starting transfers between devices: 33.8 us -> 0 us
  other arithmetic: 19.5 us -> 0.17 us
  between operations: 14.5 us -> 0.76 us
    pallas_call x0 -> x7, Pallas kernels: none -> 154 us  [the longest x1 37.5 us: backward(): pl.pallas_call(backward_kernel, grid=(S // ST,), out_shape=jax.ShapeDtype...]
    dot_general x5 -> x0, matrix products: 133 us -> none  [the longest x1 88.6 us: forward_rows(): lax.dot_general(factors, load_rows, (((1,), (1,)), ((), ())), preferred_e...]
    psum x2 -> x0, waiting for transfers between devices: 130 us -> none  [the longest x1 81.7 us: softmax_part(): loss_sum = lax.psum(partial_loss, 'cp')]
    all_to_all x1 -> x0, blocking collectives: 55.3 us -> none  [per_device(): lax.all_to_all(spread(partials[0]), 'cp', split_axis=1, concat_axis=1, ti...]
    scatter x4 -> x0, local copies, waits for them, and re-layouts: 49.5 us -> none  [spread(): jnp.zeros(shape, values.dtype).at[place_at].set(values, mode='drop')]
    psum x2 -> x0, blocking collectives: 36.5 us -> none  [the longest x1 23.9 us: reduce_scen(): lat_sum, thr_sum, expo_sum = lax.psum((lat_part, thr_part, expo_part), 'sc')]
    all_to_all x6 -> x0, starting transfers between devices: 33.7 us -> none  [the longest x1 7.49 us: per_device(): lax.all_to_all(spread(partials[2]), 'cp', split_axis=1, concat_axis=1, ti...]
    gather x3 -> x0, local copies, waits for them, and re-layouts: 25.6 us -> none  [the longest x1 12.9 us: per_device(): limit_rows = limits_in[fetch_at]]
  transfers between devices with their start and end apart: 9 -> 0, of which waited for: 5 -> 0; matrix products, arithmetic and copies ran while one was open for 17% -> 0% of each run, Pallas kernels for 0% -> 0%
where the time goes in v1:
time: 174 us; the launch traced here: 172 us
  Pallas kernels  154 us (89%)
  local copies, waits for them, and re-layouts  17.6 us (10%)
    pallas_call x1, Pallas kernels, backward(): pl.pallas_call(backward_kernel, grid=(S // ST,), out_shape=jax.ShapeDtype...  37.5 us
    pallas_call x1, Pallas kernels, forward(): pl.pallas_call(forward_kernel, grid=(S // ST,), out_shape=(jax.ShapeDtype...  32.8 us
    pallas_call x1, Pallas kernels, softmax(): pl.pallas_call(softmax_kernel, out_shape=(jax.ShapeDtypeStruct((16, S), B...  26.6 us
    pallas_call x1, Pallas kernels, exchange(): pl.pallas_call(exchange_kernel, out_shape=(jax.ShapeDtypeStruct((NCP, 16,...  22.4 us
    pallas_call x1, Pallas kernels, give_back(): pl.pallas_call(return_kernel, out_shape=(jax.ShapeDtypeStruct((32, ROWS),...  17.1 us
    pallas_call x1, Pallas kernels, add_up(): pl.pallas_call(add_kernel, out_shape=jax.ShapeDtypeStruct((40, CAP + 384)...  15.3 us
    unnamed x21, local copies, waits for them, and re-layouts  11.7 us

profile of v1, /device:TPU:0, one launch (start us, length us, event | category | flops | bytes accessed | tf_op | source)
XLA Modules:
  0.0 172.4 jit_solution(13543240725553925592)
XLA Ops:
  0.7 1.3 broadcast_in_dim.5.aversion
  2.0 0.8 concatenate.9
  2.9 1.2 concatenate.8
  4.1 0.1 copy.11
  4.3 0.2 maximum_bitcast_fusion
  4.4 1.7 reshape.30.small
  6.1 22.4 %exchange.1 = (bf16[16,16,16,256]{3,2,1,0:T(8,128)(2,1)}, bf16[16,16,256]{2,1,0:T(8,128)(2,1)}) custom-call(bf16[16,16,16,256]{3,2,1,0:T(8,128)(2,1)} %bitcast.14, bf16[16,16,256]{2,1,0:T(8,128)(2,1)} %reshape.30.small), custom_call_target="tpu_custom_call" | custom-call | tf_op jit(solution)/shard_map/exchange/pallas_call | solution.py:124
  28.5 0.9 copy-done.5
  29.4 32.8 %forward.1 = (bf16[2176,4096]{1,0:T(8,128)(2,1)}, f32[8,4096]{1,0:T(8,128)S(1)}, bf16[2432,256]{1,0:T(8,128)(2,1)S(1)}, f32[2176,128]{1,0:T(8,128)S(1)}, f32[217...) custom-call(s32[16]{0:T(128)S(1)} %copy-done.7, bf16[16,256,256]{2,1,0:T(8,128)(2,1)} %bitcast.15, ...), custom_call_target="tpu_custom_call" | custom-call | tf_op jit(solution)/shard_map/forward/pallas_call | solution.py:193
  62.2 0.8 copy-done.2
  63.1 0.7 copy-done.6
  63.7 26.6 %softmax.1 = (bf16[16,4096]{1,0:T(8,128)(2,1)}, f32[8,128]{1,0:T(8,128)}) custom-call(f32[8,4096]{1,0:T(8,128)} %copy-done.6, f32[8,128]{1,0:T(8,128)} %broadcast_in_dim.5.aversion), custom_call_target="tpu_custom_call" | custom-call | tf_op jit(solution)/shard_map/softmax/pallas_call | solution.py:321
  90.3 1.0 copy-done.3
  91.4 0.9 copy-done.4
  92.3 37.5 %backward.1.grads = f32[8,40,2176]{2,1,0:T(8,128)} custom-call(bf16[2432,256]{1,0:T(8,128)(2,1)S(1)} %get-tuple-element.21.comp, f32[2176,128]{1,0:T(8,128)S(1)} %get-tuple-element.22.shift, f32[2176,128]{1,0:T(8,128)S(1)} %get-tuple-element.23.slope, bf16[2176,128]{1,0:T(8,128)(2,1)S(1)} %copy-done.3, bf16[4096,256]{1,0:T(8,128)(2,1)} %factors.3, ...), custom_call_target="tpu_custom_call" | custom-call | tf_op jit(solution)/shard_map/backward/pallas_call | solution.py:406
  129.8 1.8 %copy-done = f32[8,40,2176]{2,1,0:T(8,128)S(1)} copy-done((f32[8,40,2176]{2,1,0:T(8,128)S(1)}, f32[8,40,2176]{2,1,0:T(8,128)}, u32[]{:S(2)}) %copy-start) | copy-done | bytes 2785304
  131.6 15.3 %add_up.1.full = f32[40,2560]{1,0:T(8,128)S(1)} custom-call(f32[8,40,2176]{2,1,0:T(8,128)S(1)} %copy-done), custom_call_target="tpu_custom_call" | custom-call | tf_op jit(solution)/shard_map/add_up/pallas_call | solution.py:500
  146.9 0.7 copy-done.1
  147.6 2.2 %place.1 = (bf16[16,32,256]{2,1,0:T(8,128)(2,1)}, f32[16,8,256]{2,1,0:T(8,128)}) custom-call(s32[16]{0:T(128)} %lengths.3, f32[40,2560]{1,0:T(8,128)} %copy-done.1), custom_call_target="tpu_custom_call" | custom-call | tf_op jit(solution)/shard_map/place/pallas_call | solution.py:536
  149.8 0.6 slice_reduce_fusion
  150.5 17.1 %give_back.1 = (f32[32,4096]{1,0:T(8,128)}, f32[1,4096]{1,0:T(1,128)}, f32[8,1,4096]{2,1,0:T(1,128)}) custom-call(bf16[16,32,256]{2,1,0:T(8,128)(2,1)} %get-tuple-element.28.pack_l, f32[16,8,256]{2,1,0:T(8,128)} %get-tuple-element.29.pack_s), custom_call_target="tpu_custom_call" | custom-call | tf_op jit(solution)/shard_map/give_back/pallas_call | solution.py:621
  167.6 1.6 copy.15
  169.2 1.9 %copy.18 = f32[4096,32]{0,1:T(8,128)} copy(f32[4096,32]{0,1:T(8,128)} %bitcast.16) | data formatting | bytes 1048576
  171.1 1.3 copy.19
  (14 shorter events, 0.1 us)
Async XLA Ops:
  4.4 24.1 %copy-start.7 = (s32[16]{0:T(128)S(1)}, s32[16]{0:T(128)}, u32[]{:S(2)}) copy-start(s32[16]{0:T(128)} %lengths.3) | copy-start | bytes 196
  28.5 0.9 copy-start.5
  62.2 0.8 copy-start.2
  63.1 0.7 copy-start.6
  90.3 1.1 copy-start.3
  91.4 0.9 copy-start.4
  129.8 1.8 %copy-start = (f32[8,40,2176]{2,1,0:T(8,128)S(1)}, f32[8,40,2176]{2,1,0:T(8,128)}, u32[]{:S(2)}) copy-start(f32[8,40,2176]{2,1,0:T(8,128)} %backward.1.grads) | copy-start | bytes 8355844
  131.6 18.2 %copy-start.8 = (f32[8,128]{1,0:T(8,128)S(1)}, f32[8,128]{1,0:T(8,128)}, u32[]{:S(2)}) copy-start(f32[8,128]{1,0:T(8,128)} %get-tuple-element.33) | copy-start | bytes 12292
  146.9 0.8 copy-start.1

commit v2 on v0

v2 whole, which is shorter than its diff:
```python
import math

import jax
import jax.numpy as jnp
from jax import lax
from jax.experimental import pallas as pl
from jax.experimental.pallas import tpu as pltpu
from jax.sharding import PartitionSpec as P

MESH = pl.DeviceIdType.MESH
NCP = 16
NSC = 8
F = 256
ROWS = 4096
S = 4096
CAP = 2176
SEG = ROWS // NCP
LIVE = 32768
SCEN = 32768
ST = 512
CHUNKS = ((0, 768), (768, 768), (1536, 640))
ROOT_HALF = 0.7071067811865476
LOG2E = 1.4426950408889634
FAR = -3.1
TAIL = (-0.750217616, 0.756257034, -1.37553279, 0.0025935648)
BF = jnp.bfloat16
F32 = jnp.float32


def spots(lengths_ref, position):
    start = jnp.int32(0)
    out = []
    for block in range(NCP):
        live = lengths_ref[block]
        tiles = (live + 15) // 16
        offset = (position - block + NCP) % NCP
        out.append((start, offset, live))
        start = start + (tiles - offset + 15) // 16
    return out


def exchange_kernel(tiles, small, got, got_small, sends, recvs, sends_s, recvs_s, sends_b, recvs_b, own):
    me = lax.axis_index("cp")
    sc = lax.axis_index("sc")
    core = sc % 2
    sibling = sc + 1 - 2 * core
    barrier = pltpu.get_barrier_semaphore()

    def greet(k, _):
        pl.semaphore_signal(barrier, inc=1, device_id=((me + k) % NCP, sc), device_id_type=MESH)
        return 0

    lax.fori_loop(1, NCP, greet, 0)
    pl.semaphore_signal(barrier, inc=1, device_id=(me, sibling), device_id_type=MESH)
    pl.semaphore_wait(barrier, NCP)

    half = pl.ds(core * 8, 8)

    def row_copy(k):
        peer = (me + k) % NCP
        return pltpu.make_async_remote_copy(
            src_ref=tiles.at[half, (peer - me + NCP) % NCP],
            dst_ref=got.at[me, half],
            send_sem=sends.at[k],
            recv_sem=recvs.at[k],
            device_id=(peer, sc),
            device_id_type=MESH,
        )

    def small_copy(k):
        peer = (me + k) % NCP
        return pltpu.make_async_remote_copy(
            src_ref=small.at[(peer - me + NCP) % NCP],
            dst_ref=got_small.at[me],
            send_sem=sends_s.at[k],
            recv_sem=recvs_s.at[k],
            device_id=(peer, sc),
            device_id_type=MESH,
        )

    def forward(k):
        source = (me - k + NCP) % NCP
        return pltpu.make_async_remote_copy(
            src_ref=got.at[source, half],
            dst_ref=got.at[source, half],
            send_sem=sends_b.at[k],
            recv_sem=recvs_b.at[k],
            device_id=(me, sibling),
            device_id_type=MESH,
        )

    def start(k, _):
        row_copy(k).start()
        small_copy(k).start()
        return 0

    lax.fori_loop(1, NCP, start, 0)
    mine = pltpu.make_async_copy(tiles.at[:, 0], got.at[me], own.at[0])
    mine.start()
    mine_small = pltpu.make_async_copy(small.at[0], got_small.at[me], own.at[1])
    mine_small.start()

    def pass_on(k, _):
        row_copy(k).wait_recv()
        forward(k).start()
        return 0

    lax.fori_loop(1, NCP, pass_on, 0)
    mine.wait()
    mine_small.wait()

    def finish(k, _):
        row_copy(k).wait_send()
        small_copy(k).wait()
        forward(k).wait()
        return 0

    lax.fori_loop(1, NCP, finish, 0)


def exchange(tiles, small):
    any_spec = pl.BlockSpec(memory_space=pl.ANY)
    return pl.pallas_call(
        exchange_kernel,
        out_shape=(
            jax.ShapeDtypeStruct((NCP, 16, 16, F), BF),
            jax.ShapeDtypeStruct((NCP, 16, SEG), BF),
        ),
        in_specs=[any_spec] * 2,
        out_specs=[any_spec] * 2,
        scratch_shapes=[pltpu.SemaphoreType.DMA((NCP,))] * 6 + [pltpu.SemaphoreType.DMA((2,))],
        compiler_params=pltpu.CompilerParams(collective_id=0, has_side_effects=True),
        name="exchange",
    )(tiles, small)


def double_cdf(u):
    far = TAIL[3]
    for coef in TAIL[2::-1]:
        far = far * u + coef
    return jnp.where(u < FAR, jnp.exp2(far), 1.0 + lax.erf(u))


def run(first, last, act):
    def body(k, _):
        act(k)
        return 0

    lax.fori_loop(first, last, body, 0)


def compact_kernel(lengths, got, got_small, comp, shift, slope, expo, expo_t, wide):
    comp[...] = jnp.zeros_like(comp)
    wide[...] = jnp.zeros_like(wide)
    index = lax.broadcasted_iota(jnp.int32, (SEG, 128), 0)
    lane = lax.broadcasted_iota(jnp.int32, (SEG, 128), 1)
    for block, (start, offset, live) in enumerate(spots(lengths, lax.axis_index("cp"))):
        at = pl.ds(pl.multiple_of(start * 16, 16), SEG)
        comp[at, :] = got[block]
        part = got_small[block].astype(F32)
        part = jnp.concatenate([part, jnp.zeros((112, SEG), F32)], axis=0).T
        row = (offset + 16 * (index // 16)) * 16 + index % 16
        keep = (row < live) | (lane >= 8)
        wide[at, :] = jnp.where(keep, part, 0.0)

    def scale(i, _):
        at = pl.ds(pl.multiple_of(i * 128, 128), 128)
        rows = comp[at, :].astype(F32)
        total = jnp.sum(rows * rows, axis=1, keepdims=True)
        by = lax.rsqrt(1.0 + total) * ROOT_HALF
        slope[at, :] = jnp.broadcast_to(by, (128, 128))
        part = wide[at, :]
        shift[at, :] = jnp.broadcast_to(part[:, 8:9] * by, (128, 128))
        expo[at, :] = part.astype(BF)
        expo_t[:, at] = part.T[0:16, :].astype(BF)
        return 0

    lax.fori_loop(0, CAP // 128, scale, 0)


def compact(lengths, got, got_small):
    vmem = pl.BlockSpec(memory_space=pltpu.VMEM)
    return pl.pallas_call(
        compact_kernel,
        out_shape=(
            jax.ShapeDtypeStruct((CAP + SEG, F), BF),
            jax.ShapeDtypeStruct((CAP, 128), F32),
            jax.ShapeDtypeStruct((CAP, 128), F32),
            jax.ShapeDtypeStruct((CAP, 128), BF),
            jax.ShapeDtypeStruct((16, CAP), BF),
        ),
        in_specs=[pl.BlockSpec(memory_space=pltpu.SMEM), vmem, vmem],
        out_specs=[vmem] * 5,
        scratch_shapes=[pltpu.VMEM((CAP + SEG, 128), F32)],
        name="compact",
    )(lengths, got, got_small)


def main_kernel(
    comp, shift, slope, expo, expo_t, factors, aversion, full, risk,
    prob, loss, parts, mine, every, stats, weights, turned,
    expo_acc, dates, dates_in, date_sum, date_all,
    load_acc, lat_acc, thr_acc, grads, pair, sum_l, near_l, thr_line, thr_pair, thr_sum, thr_near,
    sends, recvs, sends_g, recvs_g, sends_z, recvs_z, sends_d, recvs_d, sends_e, recvs_e,
    sends_a, recvs_a, sends_b, recvs_b, sends_t, recvs_t,
):
    me = lax.axis_index("cp")
    sc = lax.axis_index("sc")
    core = sc % 2
    z = sc // 2
    sibling = sc + 1 - 2 * core
    width = S // NCP
    barrier = pltpu.get_barrier_semaphore()
    run(1, NCP, lambda k: pl.semaphore_signal(barrier, inc=1, device_id=((me + k) % NCP, sc), device_id_type=MESH))
    run(1, NSC, lambda k: pl.semaphore_signal(barrier, inc=1, device_id=(me, (sc + k) % NSC), device_id_type=MESH))

    def remote(src, dst, send, recv, to):
        return pltpu.make_async_remote_copy(
            src_ref=src, dst_ref=dst, send_sem=send, recv_sem=recv, device_id=to, device_id_type=MESH
        )

    def latent(first, count, cols):
        rows = pl.ds(first, count)
        project = lax.dot_general(
            comp[rows, :], factors[cols, :], (((1,), (1,)), ((), ())), preferred_element_type=F32
        )
        a = jnp.concatenate([shift[rows, :]] * (ST // 128), axis=1)
        b = jnp.concatenate([slope[rows, :]] * (ST // 128), axis=1)
        return a - project * b

    def ahead(step):
        cols = pl.ds(pl.multiple_of(step * ST, ST), ST)
        for first, count in CHUNKS:
            prob[pl.ds(first, count), cols] = double_cdf(latent(first, count, cols)).astype(BF)
        loss[:, cols] = jnp.dot(expo_t[...], prob[:, cols], preferred_element_type=F32)[0:8, :]

    run(0, S // ST, ahead)
    pl.semaphore_wait(barrier, NCP + NSC - 2)

    def part_of(position):
        return pl.ds(pl.multiple_of(position * width, width), width)

    def scatter(k):
        peer = (me + k) % NCP
        return remote(loss.at[:, part_of(peer)], parts.at[me], sends.at[k], recvs.at[k], (peer, sc))

    def gather(k):
        return remote(mine, every.at[:, part_of(me)], sends_g.at[k], recvs_g.at[k], ((me + k) % NCP, sc))

    def share(k):
        return remote(stats.at[sc], stats.at[sc], sends_z.at[k], recvs_z.at[k], (me, (sc + k) % NSC))

    run(1, NCP, lambda k: scatter(k).start())
    parts[me] = loss[:, part_of(me)]
    at_date = lax.broadcasted_iota(jnp.int32, (8, 128), 0)
    averse = jnp.zeros((8, 128), F32)
    for t in range(8):
        averse = jnp.where(at_date == t, aversion[t], averse)
    run(1, NCP, lambda k: scatter(k).wait_recv())
    total = parts[0]
    for i in range(1, NCP):
        total = total + parts[i]
    score = jnp.concatenate([averse] * (width // 128), axis=1) * (total * (0.5 / LIVE))
    mine[...] = score
    run(1, NCP, lambda k: gather(k).start())
    every[:, part_of(me)] = score
    run(1, NCP, lambda k: gather(k).wait_recv())
    scores = every[...]
    top = jnp.max(scores, axis=1, keepdims=True)
    mass = jnp.sum(jnp.exp(scores - top), axis=1, keepdims=True)
    stats[sc, 0:8, :] = jnp.broadcast_to(top, (8, 128))
    stats[sc, 8:16, :] = jnp.broadcast_to(mass, (8, 128))
    run(1, NSC, lambda k: share(k).start())
    run(1, NSC, lambda k: share(k).wait_recv())
    best = stats[0, 0:8, :]
    for i in range(1, NSC):
        best = jnp.maximum(best, stats[i, 0:8, :])
    heap = jnp.zeros((8, 128), F32)
    for i in range(NSC):
        heap = heap + stats[i, 8:16, :] * jnp.exp(stats[i, 0:8, :] - best)
    final = jnp.exp(every[...] - best[:, 0:1]) / heap[:, 0:1]
    weights[...] = jnp.concatenate([final, jnp.zeros((8, S), F32)], axis=0).astype(BF)
    risk[...] = (best + jnp.log(heap / SCEN)) / averse
    run(1, NCP, lambda k: scatter(k).wait_send())
    run(1, NCP, lambda k: gather(k).wait_send())
    run(1, NSC, lambda k: share(k).wait_send())

    expo_acc[...] = jnp.zeros_like(expo_acc)

    def expose(step):
        cols = pl.ds(pl.multiple_of(step * ST, ST), ST)
        turned[:, 0:16] = weights[:, cols].astype(F32).T.astype(BF)
        expo_acc[...] += jnp.dot(prob[:, cols], turned[:, 0:16], preferred_element_type=F32)

    run(0, S // ST, expose)
    for i in range(CAP // 128):
        block = jnp.concatenate(
            [expo_acc[128 * i : 128 * (i + 1), :], jnp.zeros((128, 112), F32)], axis=1
        ).T
        for j in range(NSC):
            dates[j, :, 128 * i : 128 * (i + 1)] = block[j : j + 1, :] * (0.5 / LIVE)

    def date_out(k):
        peer = (sc + k) % NSC
        return remote(dates.at[peer], dates_in.at[k], sends_d.at[k], recvs_d.at[k], (me, peer))

    def date_share(k):
        return remote(date_sum, date_all.at[sc], sends_e.at[k], recvs_e.at[k], (me, (sc + k) % NSC))

    run(1, NSC, lambda k: date_out(k).start())

    def pair_copy(c, k):
        first, count = CHUNKS[c]
        at = pl.ds(first, count)
        return remote(
            grads.at[((z + k) % 4) * 2 + 1 - core, :, at], pair.at[k, :, at],
            sends_a.at[c, k], recvs_a.at[c, k], (me, sibling),
        )

    def thr_pair_copy(c):
        at = pl.ds(*CHUNKS[c])
        return remote(thr_line.at[:, at], thr_pair.at[:, at], sends_a.at[c, 4], recvs_a.at[c, 4], (me, sibling))

    def near_copy(c, k):
        at = pl.ds(*CHUNKS[c])
        return remote(
            sum_l.at[k, :, at], near_l.at[k, :, at],
            sends_b.at[c, k], recvs_b.at[c, k], (me, ((z + k) % 4) * 2 + core),
        )

    def thr_near_copy(c, k):
        at = pl.ds(*CHUNKS[c])
        return remote(
            thr_sum.at[:, at], thr_near.at[k, :, at],
            sends_t.at[c, k], recvs_t.at[c, k], (me, ((z + k) % 4) * 2 + core),
        )

    def back_steps(c, low, high):
        first, count = CHUNKS[c]
        rows = pl.ds(first, count)
        acc = pl.ds(0, count)

        def step(i):
            cols = pl.ds(pl.multiple_of(i * ST, ST), ST)
            pull = jnp.dot(expo[rows, 0:16], weights[:, cols], preferred_element_type=F32)
            u = latent(first, count, cols)
            heavy = pull * jnp.exp2(u * u * (-LOG2E))
            lat = heavy * u
            lat_sum = lat[:, 0:128]
            thr_part = heavy[:, 0:128]
            for k in range(1, ST // 128):
                lat_sum = lat_sum + lat[:, k * 128 : (k + 1) * 128]
                thr_part = thr_part + heavy[:, k * 128 : (k + 1) * 128]
            lat_acc[acc, :] += lat_sum
            thr_acc[acc, :] += thr_part
            load_acc[acc, :] += jnp.dot(heavy.astype(BF), factors[cols, :], preferred_element_type=F32)

        run(low, high, step)

    def fold(c):
        first, count = CHUNKS[c]
        scale = 1.0 / (LIVE * math.sqrt(2.0 * math.pi))

        def one(i):
            rows = pl.ds(pl.multiple_of(first + i * 128, 128), 128)
            acc = pl.ds(pl.multiple_of(i * 128, 128), 128)
            by = slope[rows, 0:1] * math.sqrt(2.0)
            lat = jnp.sum(lat_acc[acc, :], axis=1, keepdims=True) * (scale * math.sqrt(2.0))
            thr = jnp.sum(thr_acc[acc, :], axis=1, keepdims=True) * scale * by
            grad = -(load_acc[acc, :] * (scale * by)) - (lat * by * by) * comp[rows, :].astype(F32)
            flat = grad.T
            for j in range(NSC):
                grads[j, :, rows] = flat[32 * j : 32 * (j + 1), :]
            thr_line[:, rows] = jnp.broadcast_to(thr, (128, 128)).T[0:1, :]

        run(0, count // 128, one)
        for k in (2, 1, 3, 0):
            pair_copy(c, k).start()
        thr_pair_copy(c).start()

    def pair_up(c):
        first, count = CHUNKS[c]
        at = pl.ds(first, count)
        for k in (2, 1, 3):
            pair_copy(c, k).wait_recv()
            sum_l[k, :, at] = (grads[((z + k) % 4) * 2 + core, :, at] + pair[k, :, at]).astype(BF)
            near_copy(c, k).start()
        thr_pair_copy(c).wait_recv()
        thr_sum[:, at] = thr_line[:, at] + thr_pair[:, at]
        for k in (2, 1, 3):
            thr_near_copy(c, k).start()
        pair_copy(c, 0).wait_recv()

    def near_up(c):
        first, count = CHUNKS[c]
        at = pl.ds(first, count)
        held = grads[sc, :, at] + pair[0, :, at]
        thr = thr_sum[:, at]
        for k in (1, 3, 2):
            near_copy(c, k).wait_recv()
            thr_near_copy(c, k).wait_recv()
            held = held + near_l[k, :, at].astype(F32)
            thr = thr + thr_near[k, :, at]
        full[0:32, at] = held
        full[40:41, at] = thr

    full[:, CAP:] = jnp.zeros((48, 384), F32)
    full[41:48, 0:CAP] = jnp.zeros((7, CAP), F32)
    steps = S // ST
    for c in range(len(CHUNKS)):
        load_acc[...] = jnp.zeros_like(load_acc)
        lat_acc[...] = jnp.zeros_like(lat_acc)
        thr_acc[...] = jnp.zeros_like(thr_acc)
        back_steps(c, 0, steps // 2)
        if c == 0:
            run(1, NSC, lambda k: date_out(k).wait_recv())
            line = dates[sc]
            for k in range(1, NSC):
                line = line + dates_in[k]
            date_sum[...] = line
            run(1, NSC, lambda k: date_share(k).start())
            date_all[sc] = line
        else:
            pair_up(c - 1)
        back_steps(c, steps // 2, steps)
        if c:
            near_up(c - 1)
        fold(c)
    last = len(CHUNKS) - 1
    run(1, NSC, lambda k: date_share(k).wait_recv())
    for j in range(NSC):
        full[32 + j : 33 + j, 0:CAP] = date_all[j]
    pair_up(last)
    run(1, NSC, lambda k: (date_out(k).wait_send(), date_share(k).wait_send()))
    near_up(last)
    for c in range(len(CHUNKS)):
        for k in range(4):
            pair_copy(c, k).wait_send()
        thr_pair_copy(c).wait_send()
        for k in range(1, 4):
            near_copy(c, k).wait_send()
            thr_near_copy(c, k).wait_send()


def main(comp, shift, slope, expo, expo_t, factors, aversion):
    vmem = pl.BlockSpec(memory_space=pltpu.VMEM)
    dma = pltpu.SemaphoreType.DMA
    parts = len(CHUNKS)
    most = max(count for _, count in CHUNKS)
    return pl.pallas_call(
        main_kernel,
        out_shape=(
            jax.ShapeDtypeStruct((48, CAP + 384), F32),
            jax.ShapeDtypeStruct((8, 128), F32),
        ),
        in_specs=[vmem] * 6 + [pl.BlockSpec(memory_space=pltpu.SMEM)],
        out_specs=[vmem] * 2,
        scratch_shapes=[
            pltpu.VMEM((CAP, S), BF),
            pltpu.VMEM((8, S), F32),
            pltpu.VMEM((NCP, 8, S // NCP), F32),
            pltpu.VMEM((8, S // NCP), F32),
            pltpu.VMEM((8, S), F32),
            pltpu.VMEM((NSC, 16, 128), F32),
            pltpu.VMEM((16, S), BF),
            pltpu.VMEM((ST, 128), BF),
            pltpu.VMEM((CAP, 16), F32),
            pltpu.VMEM((NSC, 1, CAP), F32),
            pltpu.VMEM((NSC, 1, CAP), F32),
            pltpu.VMEM((1, CAP), F32),
            pltpu.VMEM((NSC, 1, CAP), F32),
            pltpu.VMEM((most, F), F32),
            pltpu.VMEM((most, 128), F32),
            pltpu.VMEM((most, 128), F32),
            pltpu.VMEM((NSC, 32, CAP), F32),
            pltpu.VMEM((4, 32, CAP), F32),
            pltpu.VMEM((4, 32, CAP), BF),
            pltpu.VMEM((4, 32, CAP), BF),
            pltpu.VMEM((1, CAP), F32),
            pltpu.VMEM((1, CAP), F32),
            pltpu.VMEM((1, CAP), F32),
            pltpu.VMEM((4, 1, CAP), F32),
            dma((NCP,)),
            dma((NCP,)),
            dma((NCP,)),
            dma((NCP,)),
            dma((NSC,)),
            dma((NSC,)),
            dma((NSC,)),
            dma((NSC,)),
            dma((NSC,)),
            dma((NSC,)),
            dma((parts, 5)),
            dma((parts, 5)),
            dma((parts, 4)),
            dma((parts, 4)),
            dma((parts, 4)),
            dma((parts, 4)),
        ],
        compiler_params=pltpu.CompilerParams(
            collective_id=1, has_side_effects=True, vmem_limit_bytes=58 * 2**20
        ),
        name="main",
    )(comp, shift, slope, expo, expo_t, factors, aversion)


def place_kernel(lengths, full, pack):
    lane = lax.broadcasted_iota(jnp.int32, (48, SEG), 1)
    for block, (start, offset, live) in enumerate(spots(lengths, lax.axis_index("cp"))):
        at = pl.ds(pl.multiple_of((start // 8) * 128, 128), 384)
        piece = pltpu.roll(full[:, at], (24 - start % 8) * 16 % 384, 1)[:, 0:SEG]
        row = (offset + 16 * (lane // 16)) * 16 + lane % 16
        pack[block] = jnp.where(row < live, piece, 0.0).astype(BF)


def place(lengths, full):
    vmem = pl.BlockSpec(memory_space=pltpu.VMEM)
    return pl.pallas_call(
        place_kernel,
        out_shape=jax.ShapeDtypeStruct((NCP, 48, SEG), BF),
        in_specs=[pl.BlockSpec(memory_space=pltpu.SMEM), vmem],
        out_specs=vmem,
        name="place",
    )(lengths, full)


def return_kernel(pack, load_out, thr_out, expo_out, back, sends, recvs):
    me = lax.axis_index("cp")
    sc = lax.axis_index("sc")
    barrier = pltpu.get_barrier_semaphore()
    run(1, NCP, lambda k: pl.semaphore_signal(barrier, inc=1, device_id=((me + k) % NCP, sc), device_id_type=MESH))
    pl.semaphore_wait(barrier, NCP - 1)

    def back_copy(k):
        peer = (me + k) % NCP
        return pltpu.make_async_remote_copy(
            src_ref=pack.at[peer],
            dst_ref=back.at[(me - peer + NCP) % NCP],
            send_sem=sends.at[k],
            recv_sem=recvs.at[k],
            device_id=(peer, sc),
            device_id_type=MESH,
        )

    run(1, NCP, lambda k: back_copy(k).start())
    back[0] = pack[me]
    run(1, NCP, lambda k: back_copy(k).wait_recv())
    group = lax.broadcasted_iota(jnp.int32, (48, 128), 1) // 16
    for g in range(2):
        for h in range(2):
            held = [back[8 * g + q, :, 128 * h : 128 * (h + 1)].astype(F32) for q in range(8)]
            for s in range(8):
                mixed = held[s]
                for q in range(8):
                    if q != s:
                        turned = pltpu.roll(held[q], (16 * (q - s)) % 128, 1)
                        mixed = jnp.where(group == q, turned, mixed)
                tile = 2 * (8 * h + s) + g
                at = slice(128 * tile, 128 * (tile + 1))
                load_out[:, at] = mixed[0:32, :]
                expo_out[:, at] = mixed[32:40, :]
                thr_out[:, at] = mixed[40:41, :]
    run(1, NCP, lambda k: back_copy(k).wait_send())


def give_back(pack):
    vmem = pl.BlockSpec(memory_space=pltpu.VMEM)
    return pl.pallas_call(
        return_kernel,
        out_shape=(
            jax.ShapeDtypeStruct((32, ROWS), F32),
            jax.ShapeDtypeStruct((1, ROWS), F32),
            jax.ShapeDtypeStruct((NSC, ROWS), F32),
        ),
        in_specs=[vmem],
        out_specs=[vmem] * 3,
        scratch_shapes=[
            pltpu.VMEM((NCP, 48, SEG), BF),
            pltpu.SemaphoreType.DMA((NCP,)),
            pltpu.SemaphoreType.DMA((NCP,)),
        ],
        compiler_params=pltpu.CompilerParams(collective_id=2, has_side_effects=True),
        name="give_back",
    )(pack)


def per_device(factors, loadings, thresholds, exposures, aversion, lengths):
    tiles = loadings.reshape(16, NCP, 16, F)
    small = jnp.concatenate(
        [exposures.T, thresholds[None, :], jnp.zeros((7, ROWS), BF)], axis=0
    )
    small = small.reshape(16, 16, NCP, 16).transpose(2, 0, 1, 3).reshape(NCP, 16, SEG)
    got, got_small = exchange(tiles, small)
    rows = compact(lengths, got.reshape(NCP, SEG, F), got_small)
    full, risk = main(*rows, factors, aversion)
    load, thr, dates = give_back(place(lengths, full))
    return (load.T, thr.reshape(ROWS), dates.T, risk[:, 0])


def solution(mesh):
    in_specs = (P("sc", None), P("cp", None), P("cp"), P("cp", None), P(), P())
    out_specs = (P("cp", "sc"), P("cp"), P("cp", None), P())
    return jax.shard_map(
        per_device, mesh=mesh, in_specs=in_specs, out_specs=out_specs, check_vma=False
    )
```

time: 582 us -> 146 us (0.25); the launches traced: 573 us -> 146 us
  waiting for transfers between devices: 144 us -> 0 us
  Pallas kernels: 0 us -> 135 us
  matrix products: 133 us -> 0 us
  local copies, waits for them, and re-layouts: 124 us -> 9.99 us
  blocking collectives: 105 us -> 0 us
  starting transfers between devices: 33.8 us -> 0 us
  other arithmetic: 19.5 us -> 0.17 us
  between operations: 14.5 us -> 0.7 us
    pallas_call x0 -> x5, Pallas kernels: none -> 135 us  [the longest x1 88.8 us: main(): pl.pallas_call(main_kernel, out_shape=(jax.ShapeDtypeStruct((48, CAP + 38...]
    dot_general x5 -> x0, matrix products: 133 us -> none  [the longest x1 88.6 us: forward_rows(): lax.dot_general(factors, load_rows, (((1,), (1,)), ((), ())), preferred_e...]
    psum x2 -> x0, waiting for transfers between devices: 130 us -> none  [the longest x1 81.7 us: softmax_part(): loss_sum = lax.psum(partial_loss, 'cp')]
    all_to_all x1 -> x0, blocking collectives: 55.3 us -> none  [per_device(): lax.all_to_all(spread(partials[0]), 'cp', split_axis=1, concat_axis=1, ti...]
    scatter x4 -> x0, local copies, waits for them, and re-layouts: 49.5 us -> none  [spread(): jnp.zeros(shape, values.dtype).at[place_at].set(values, mode='drop')]
    psum x2 -> x0, blocking collectives: 36.5 us -> none  [the longest x1 23.9 us: reduce_scen(): lat_sum, thr_sum, expo_sum = lax.psum((lat_part, thr_part, expo_part), 'sc')]
    all_to_all x6 -> x0, starting transfers between devices: 33.7 us -> none  [the longest x1 7.49 us: per_device(): lax.all_to_all(spread(partials[2]), 'cp', split_axis=1, concat_axis=1, ti...]
    gather x3 -> x0, local copies, waits for them, and re-layouts: 25.6 us -> none  [the longest x1 12.9 us: per_device(): limit_rows = limits_in[fetch_at]]
  transfers between devices with their start and end apart: 9 -> 0, of which waited for: 5 -> 0; matrix products, arithmetic and copies ran while one was open for 17% -> 0% of each run, Pallas kernels for 0% -> 0%
where the time goes in v2:
time: 146 us
  Pallas kernels  135 us (92%)
  local copies, waits for them, and re-layouts  9.99 us (7%)
    pallas_call x1, Pallas kernels, main(): pl.pallas_call(main_kernel, out_shape=(jax.ShapeDtypeStruct((48, CAP + 38...  88.8 us
    pallas_call x1, Pallas kernels, exchange(): pl.pallas_call(exchange_kernel, out_shape=(jax.ShapeDtypeStruct((NCP, 16,...  22.4 us
    pallas_call x1, Pallas kernels, give_back(): pl.pallas_call(return_kernel, out_shape=(jax.ShapeDtypeStruct((32, ROWS),...  13.4 us
    pallas_call x1, Pallas kernels, compact(): pl.pallas_call(compact_kernel, out_shape=(jax.ShapeDtypeStruct((CAP + SEG...  8.05 us
    unnamed x3, local copies, waits for them, and re-layouts  4.76 us

profile of v2, /device:TPU:0, one launch (start us, length us, event | category | flops | bytes accessed | tf_op | source)
XLA Modules:
  0.0 145.8 jit_solution(9789913881854904230)
XLA Ops:
  0.6 0.1 pad.2.clone
  0.7 0.8 concatenate.9
  1.5 1.2 concatenate.8
  2.8 0.1 copy.11
  2.9 0.2 maximum_bitcast_fusion
  3.1 1.7 %reshape.26.small = bf16[16,16,256]{2,1,0:T(8,128)(2,1)} reshape(bf16[16,16,16,16]{3,2,1,0:T(8,128)(2,1)S(1)} %maximum_bitcast_fusion) | data formatting | bytes 262144 | tf_op jit(solution)/shard_map/reshape | solution.py:592
  4.8 22.4 %exchange.1 = (bf16[16,16,16,256]{3,2,1,0:T(8,128)(2,1)}, bf16[16,16,256]{2,1,0:T(8,128)(2,1)}) custom-call(bf16[16,16,16,256]{3,2,1,0:T(8,128)(2,1)} %bitcast.11, bf16[16,16,256]{2,1,0:T(8,128)(2,1)} %reshape.26.small), custom_call_target="tpu_custom_call" | custom-call | tf_op jit(solution)/shard_map/exchange/pallas_call | solution.py:123
  27.2 8.1 %compact.1 = (bf16[2432,256]{1,0:T(8,128)(2,1)}, f32[2176,128]{1,0:T(8,128)}, f32[2176,128]{1,0:T(8,128)}, bf16[2176,128]{1,0:T(8,128)(2,1)}, bf16[16,2176]{1,0:T(8,128)(2,1)}) custom-call(s32[16]{0:T(128)} %lengths.3, bf16[16,256,256]{2,1,0:T(8,128)(2,1)} %bitcast.10, bf16[16,16,256]{2,1,0:T(8,128)(2,1)} %get-tuple-element.17.got_small), custom_call_target="tpu_custom_call" | custom-call | tf_op jit(solution)/shard_map/compact/pallas_call | solution.py:183
  35.3 88.8 %main.1 = (f32[48,2560]{1,0:T(8,128)}, f32[8,128]{1,0:T(8,128)}) custom-call(bf16[2432,256]{1,0:T(8,128)(2,1)} %get-tuple-element.18.comp, f32[2176,128]{1,0:T(8,128)} %get-tuple-element.19.shift, f32[2176,128]{1,0:T(8,128)} %get-tuple-element.20.slope, bf16[2176,128]{1,0:T(8,128)(2,1)} %get-tuple-element.21.expo, ...), custom_call_target="tpu_custom_call" | custom-call | tf_op jit(solution)/shard_map/main/pallas_call | solution.py:450
  124.0 2.3 %place.1.pack = bf16[16,48,256]{2,1,0:T(8,128)(2,1)} custom-call(s32[16]{0:T(128)} %lengths.3, f32[48,2560]{1,0:T(8,128)} %get-tuple-element.23.full), custom_call_target="tpu_custom_call" | custom-call | tf_op jit(solution)/shard_map/place/pallas_call | solution.py:518
  126.3 1.3 slice_reduce_fusion
  127.6 13.4 %give_back.1 = (f32[32,4096]{1,0:T(8,128)}, f32[1,4096]{1,0:T(1,128)}, f32[8,4096]{1,0:T(8,128)}) custom-call(bf16[16,48,256]{2,1,0:T(8,128)(2,1)} %place.1.pack), custom_call_target="tpu_custom_call" | custom-call | tf_op jit(solution)/shard_map/give_back/pallas_call | solution.py:568
  141.0 1.9 %copy.16 = f32[4096,32]{0,1:T(8,128)} copy(f32[4096,32]{0,1:T(8,128)} %bitcast.12) | data formatting | bytes 1048576
  142.9 1.3 copy.17
  144.2 1.6 %copy.18 = f32[4096,8]{0,1:T(8,128)} copy(f32[4096,8]{0,1:T(8,128)} %bitcast.13) | data formatting | bytes 262144
  (2 shorter events, 0.0 us)

commit v3 on v2

--- a/solution.py
+++ b/solution.py
@@ -32,10 +32,10 @@
     out = []
     for block in range(NCP):
         live = lengths_ref[block]
-        tiles = (live + 15) // 16
+        tiles = (live + 15) >> 4
         offset = (position - block + NCP) % NCP
         out.append((start, offset, live))
-        start = start + (tiles - offset + 15) // 16
+        start = start + ((tiles - offset + 15) >> 4)
     return out
 
 
@@ -197,12 +197,12 @@
 
 
 def main_kernel(
-    comp, shift, slope, expo, expo_t, factors, aversion, full, risk,
-    prob, loss, parts, mine, every, stats, weights, turned,
+    comp, shift, slope, expo, expo_t, factors, aversion, lengths, load_out, thr_out, expo_out, risk,
+    full, pack, back, prob, loss, parts, mine, every, stats, weights, turned,
     expo_acc, dates, dates_in, date_sum, date_all,
     load_acc, lat_acc, thr_acc, grads, pair, sum_l, near_l, thr_line, thr_pair, thr_sum, thr_near,
     sends, recvs, sends_g, recvs_g, sends_z, recvs_z, sends_d, recvs_d, sends_e, recvs_e,
-    sends_a, recvs_a, sends_b, recvs_b, sends_t, recvs_t,
+    sends_a, recvs_a, sends_b, recvs_b, sends_t, recvs_t, sends_c, recvs_c,
 ):
     me = lax.axis_index("cp")
     sc = lax.axis_index("sc")
@@ -267,10 +267,21 @@
     run(1, NCP, lambda k: gather(k).wait_recv())
     scores = every[...]
     top = jnp.max(scores, axis=1, keepdims=True)
-    mass = jnp.sum(jnp.exp(scores - top), axis=1, keepdims=True)
+    raised = jnp.exp(scores - top)
+    mass = jnp.sum(raised, axis=1, keepdims=True)
     stats[sc, 0:8, :] = jnp.broadcast_to(top, (8, 128))
     stats[sc, 8:16, :] = jnp.broadcast_to(mass, (8, 128))
     run(1, NSC, lambda k: share(k).start())
+    weights[...] = jnp.concatenate([raised, jnp.zeros((8, S), F32)], axis=0).astype(BF)
+
+    expo_acc[...] = jnp.zeros_like(expo_acc)
+
+    def expose(step):
+        cols = pl.ds(pl.multiple_of(step * ST, ST), ST)
+        turned[:, 0:16] = weights[:, cols].astype(F32).T.astype(BF)
+        expo_acc[...] += jnp.dot(prob[:, cols], turned[:, 0:16], preferred_element_type=F32)
+
+    run(0, S // ST, expose)
     run(1, NSC, lambda k: share(k).wait_recv())
     best = stats[0, 0:8, :]
     for i in range(1, NSC):
@@ -284,21 +295,13 @@
     run(1, NCP, lambda k: scatter(k).wait_send())
     run(1, NCP, lambda k: gather(k).wait_send())
     run(1, NSC, lambda k: share(k).wait_send())
-
-    expo_acc[...] = jnp.zeros_like(expo_acc)
-
-    def expose(step):
-        cols = pl.ds(pl.multiple_of(step * ST, ST), ST)
-        turned[:, 0:16] = weights[:, cols].astype(F32).T.astype(BF)
-        expo_acc[...] += jnp.dot(prob[:, cols], turned[:, 0:16], preferred_element_type=F32)
-
-    run(0, S // ST, expose)
+    own_scale = jnp.exp(stats[sc, 0:8, :] - best) / heap * (0.5 / LIVE)
     for i in range(CAP // 128):
         block = jnp.concatenate(
             [expo_acc[128 * i : 128 * (i + 1), :], jnp.zeros((128, 112), F32)], axis=1
         ).T
         for j in range(NSC):
-            dates[j, :, 128 * i : 128 * (i + 1)] = block[j : j + 1, :] * (0.5 / LIVE)
+            dates[j, :, 128 * i : 128 * (i + 1)] = block[j : j + 1, :] * own_scale[j : j + 1, :]
 
     def date_out(k):
         peer = (sc + k) % NSC
@@ -401,11 +404,13 @@
             thr_near_copy(c, k).wait_recv()
             held = held + near_l[k, :, at].astype(F32)
             thr = thr + thr_near[k, :, at]
-        full[0:32, at] = held
-        full[40:41, at] = thr
-
-    full[:, CAP:] = jnp.zeros((48, 384), F32)
-    full[41:48, 0:CAP] = jnp.zeros((7, CAP), F32)
+        for i in range(count // 128):
+            part = slice(128 * i, 128 * (i + 1))
+            full[first // 128 + i, 0:32, :] = held[:, part]
+            full[first // 128 + i, 40:41, :] = thr[:, part]
+
+    full[CAP // 128 :, :, :] = jnp.zeros((3, 48, 128), F32)
+    full[0 : CAP // 128, 40:48, :] = jnp.zeros((CAP // 128, 8, 128), F32)
     steps = S // ST
     for c in range(len(CHUNKS)):
         load_acc[...] = jnp.zeros_like(load_acc)
@@ -429,10 +434,27 @@
     last = len(CHUNKS) - 1
     run(1, NSC, lambda k: date_share(k).wait_recv())
     for j in range(NSC):
-        full[32 + j : 33 + j, 0:CAP] = date_all[j]
+        for i in range(CAP // 128):
+            full[i, 32 + j : 33 + j, :] = date_all[j, :, 128 * i : 128 * (i + 1)]
     pair_up(last)
     run(1, NSC, lambda k: (date_out(k).wait_send(), date_share(k).wait_send()))
     near_up(last)
+    lane = lax.broadcasted_iota(jnp.int32, (48, SEG), 1)
+    for block, (start, offset, live) in enumerate(spots(lengths, me)):
+        tile = start >> 3
+        piece = jnp.concatenate([full[tile], full[tile + 1], full[tile + 2]], axis=1)
+        part = jnp.full((48, 384), start & 7, jnp.int32)
+        for bit in (1, 2, 4):
+            piece = jnp.where(part & bit != 0, pltpu.roll(piece, 384 - 16 * bit, 1), piece)
+        row = (offset + 16 * (lane // 16)) * 16 + lane % 16
+        pack[block] = jnp.where(row < live, piece[:, 0:SEG], 0.0).astype(BF)
+
+    def back_copy(k):
+        peer = (me + k) % NCP
+        return remote(pack.at[peer], back.at[(me - peer + NCP) % NCP], sends_c.at[k], recvs_c.at[k], (peer, sc))
+
+    run(1, NCP, lambda k: back_copy(k).start())
+    back[0] = pack[me]
     for c in range(len(CHUNKS)):
         for k in range(4):
             pair_copy(c, k).wait_send()
@@ -440,9 +462,26 @@
         for k in range(1, 4):
             near_copy(c, k).wait_send()
             thr_near_copy(c, k).wait_send()
-
-
-def main(comp, shift, slope, expo, expo_t, factors, aversion):
+    run(1, NCP, lambda k: back_copy(k).wait_recv())
+    group = lax.broadcasted_iota(jnp.int32, (48, 128), 1) // 16
+    for g in range(2):
+        for h in range(2):
+            held = [back[8 * g + q, :, 128 * h : 128 * (h + 1)].astype(F32) for q in range(8)]
+            for s in range(8):
+                mixed = held[s]
+                for q in range(8):
+                    if q != s:
+                        moved = pltpu.roll(held[q], (16 * (q - s)) % 128, 1)
+                        mixed = jnp.where(group == q, moved, mixed)
+                tile = 2 * (8 * h + s) + g
+                at = slice(128 * tile, 128 * (tile + 1))
+                load_out[:, at] = mixed[0:32, :]
+                expo_out[:, at] = mixed[32:40, :]
+                thr_out[:, at] = mixed[40:41, :]
+    run(1, NCP, lambda k: back_copy(k).wait_send())
+
+
+def main(comp, shift, slope, expo, expo_t, factors, aversion, lengths):
     vmem = pl.BlockSpec(memory_space=pltpu.VMEM)
     dma = pltpu.SemaphoreType.DMA
     parts = len(CHUNKS)
@@ -450,12 +489,17 @@
     return pl.pallas_call(
         main_kernel,
         out_shape=(
-            jax.ShapeDtypeStruct((48, CAP + 384), F32),
+            jax.ShapeDtypeStruct((32, ROWS), F32),
+            jax.ShapeDtypeStruct((1, ROWS), F32),
+            jax.ShapeDtypeStruct((NSC, ROWS), F32),
             jax.ShapeDtypeStruct((8, 128), F32),
         ),
-        in_specs=[vmem] * 6 + [pl.BlockSpec(memory_space=pltpu.SMEM)],
-        out_specs=[vmem] * 2,
+        in_specs=[vmem] * 6 + [pl.BlockSpec(memory_space=pltpu.SMEM)] * 2,
+        out_specs=[vmem] * 4,
         scratch_shapes=[
+            pltpu.VMEM((CAP // 128 + 3, 48, 128), F32),
+            pltpu.VMEM((NCP, 48, SEG), BF),
+            pltpu.VMEM((NCP, 48, SEG), BF),
             pltpu.VMEM((CAP, S), BF),
             pltpu.VMEM((8, S), F32),
             pltpu.VMEM((NCP, 8, S // NCP), F32),
@@ -496,92 +540,14 @@
             dma((parts, 4)),
             dma((parts, 4)),
             dma((parts, 4)),
+            dma((NCP,)),
+            dma((NCP,)),
         ],
         compiler_params=pltpu.CompilerParams(
             collective_id=1, has_side_effects=True, vmem_limit_bytes=58 * 2**20
         ),
         name="main",
-    )(comp, shift, slope, expo, expo_t, factors, aversion)
-
-
-def place_kernel(lengths, full, pack):
-    lane = lax.broadcasted_iota(jnp.int32, (48, SEG), 1)
-    for block, (start, offset, live) in enumerate(spots(lengths, lax.axis_index("cp"))):
-        at = pl.ds(pl.multiple_of((start // 8) * 128, 128), 384)
-        piece = pltpu.roll(full[:, at], (24 - start % 8) * 16 % 384, 1)[:, 0:SEG]
-        row = (offset + 16 * (lane // 16)) * 16 + lane % 16
-        pack[block] = jnp.where(row < live, piece, 0.0).astype(BF)
-
-
-def place(lengths, full):
-    vmem = pl.BlockSpec(memory_space=pltpu.VMEM)
-    return pl.pallas_call(
-        place_kernel,
-        out_shape=jax.ShapeDtypeStruct((NCP, 48, SEG), BF),
-        in_specs=[pl.BlockSpec(memory_space=pltpu.SMEM), vmem],
-        out_specs=vmem,
-        name="place",
-    )(lengths, full)
-
-
-def return_kernel(pack, load_out, thr_out, expo_out, back, sends, recvs):
-    me = lax.axis_index("cp")
-    sc = lax.axis_index("sc")
-    barrier = pltpu.get_barrier_semaphore()
-    run(1, NCP, lambda k: pl.semaphore_signal(barrier, inc=1, device_id=((me + k) % NCP, sc), device_id_type=MESH))
-    pl.semaphore_wait(barrier, NCP - 1)
-
-    def back_copy(k):
-        peer = (me + k) % NCP
-        return pltpu.make_async_remote_copy(
-            src_ref=pack.at[peer],
-            dst_ref=back.at[(me - peer + NCP) % NCP],
-            send_sem=sends.at[k],
-            recv_sem=recvs.at[k],
-            device_id=(peer, sc),
-            device_id_type=MESH,
-        )
-
-    run(1, NCP, lambda k: back_copy(k).start())
-    back[0] = pack[me]
-    run(1, NCP, lambda k: back_copy(k).wait_recv())
-    group = lax.broadcasted_iota(jnp.int32, (48, 128), 1) // 16
-    for g in range(2):
-        for h in range(2):
-            held = [back[8 * g + q, :, 128 * h : 128 * (h + 1)].astype(F32) for q in range(8)]
-            for s in range(8):
-                mixed = held[s]
-                for q in range(8):
-                    if q != s:
-                        turned = pltpu.roll(held[q], (16 * (q - s)) % 128, 1)
-                        mixed = jnp.where(group == q, turned, mixed)
-                tile = 2 * (8 * h + s) + g
-                at = slice(128 * tile, 128 * (tile + 1))
-                load_out[:, at] = mixed[0:32, :]
-                expo_out[:, at] = mixed[32:40, :]
-                thr_out[:, at] = mixed[40:41, :]
-    run(1, NCP, lambda k: back_copy(k).wait_send())
-
-
-def give_back(pack):
-    vmem = pl.BlockSpec(memory_space=pltpu.VMEM)
-    return pl.pallas_call(
-        return_kernel,
-        out_shape=(
-            jax.ShapeDtypeStruct((32, ROWS), F32),
-            jax.ShapeDtypeStruct((1, ROWS), F32),
-            jax.ShapeDtypeStruct((NSC, ROWS), F32),
-        ),
-        in_specs=[vmem],
-        out_specs=[vmem] * 3,
-        scratch_shapes=[
-            pltpu.VMEM((NCP, 48, SEG), BF),
-            pltpu.SemaphoreType.DMA((NCP,)),
-            pltpu.SemaphoreType.DMA((NCP,)),
-        ],
-        compiler_params=pltpu.CompilerParams(collective_id=2, has_side_effects=True),
-        name="give_back",
-    )(pack)
+    )(comp, shift, slope, expo, expo_t, factors, aversion, lengths)
 
 
 def per_device(factors, loadings, thresholds, exposures, aversion, lengths):
@@ -592,8 +558,7 @@
     small = small.reshape(16, 16, NCP, 16).transpose(2, 0, 1, 3).reshape(NCP, 16, SEG)
     got, got_small = exchange(tiles, small)
     rows = compact(lengths, got.reshape(NCP, SEG, F), got_small)
-    full, risk = main(*rows, factors, aversion)
-    load, thr, dates = give_back(place(lengths, full))
+    load, thr, dates, risk = main(*rows, factors, aversion, lengths)
     return (load.T, thr.reshape(ROWS), dates.T, risk[:, 0])
 
 

time: 146 us -> 138 us (0.945)
  Pallas kernels: 135 us -> 127 us
    pallas_call x3 -> x1, Pallas kernels: 104 us -> 96.2 us  [main(): pl.pallas_call(main_kernel, out_shape=(jax.ShapeDtypeStruct((32, ROWS), F...]
where the time goes in v3:
time: 138 us
  Pallas kernels  127 us (92%)
  local copies, waits for them, and re-layouts  9.98 us (7%)
    pallas_call x1, Pallas kernels, main(): pl.pallas_call(main_kernel, out_shape=(jax.ShapeDtypeStruct((32, ROWS), F...  96.2 us
    pallas_call x1, Pallas kernels, exchange(): pl.pallas_call(exchange_kernel, out_shape=(jax.ShapeDtypeStruct((NCP, 16,...  22.4 us
    pallas_call x1, Pallas kernels, compact(): pl.pallas_call(compact_kernel, out_shape=(jax.ShapeDtypeStruct((CAP + SEG...  8.09 us
    unnamed x3, local copies, waits for them, and re-layouts  4.76 us

profile of v3, /device:TPU:0, one launch (start us, length us, event | category | flops | bytes accessed | tf_op | source)
XLA Modules:
  0.0 137.6 jit_solution(14459046333099308346)
XLA Ops:
  0.6 0.1 pad.2.clone
  0.7 0.8 concatenate.9
  1.5 1.2 concatenate.8
  2.8 0.1 copy.11
  2.9 0.2 maximum_bitcast_fusion
  3.1 1.7 %reshape.26.small = bf16[16,16,256]{2,1,0:T(8,128)(2,1)} reshape(bf16[16,16,16,16]{3,2,1,0:T(8,128)(2,1)S(1)} %maximum_bitcast_fusion) | data formatting | bytes 262144 | tf_op jit(solution)/shard_map/reshape | solution.py:558
  4.8 22.4 %exchange.1 = (bf16[16,16,16,256]{3,2,1,0:T(8,128)(2,1)}, bf16[16,16,256]{2,1,0:T(8,128)(2,1)}) custom-call(bf16[16,16,16,256]{3,2,1,0:T(8,128)(2,1)} %bitcast.11, bf16[16,16,256]{2,1,0:T(8,128)(2,1)} %reshape.26.small), custom_call_target="tpu_custom_call" | custom-call | tf_op jit(solution)/shard_map/exchange/pallas_call | solution.py:123
  27.2 8.1 %compact.1 = (bf16[2432,256]{1,0:T(8,128)(2,1)}, f32[2176,128]{1,0:T(8,128)}, f32[2176,128]{1,0:T(8,128)}, bf16[2176,128]{1,0:T(8,128)(2,1)}, bf16[16,2176]{1,0:T(8,128)(2,1)}) custom-call(s32[16]{0:T(128)} %lengths.3, bf16[16,256,256]{2,1,0:T(8,128)(2,1)} %bitcast.10, bf16[16,16,256]{2,1,0:T(8,128)(2,1)} %get-tuple-element.16.got_small), custom_call_target="tpu_custom_call" | custom-call | tf_op jit(solution)/shard_map/compact/pallas_call | solution.py:183
  35.3 96.2 %main.1 = (f32[32,4096]{1,0:T(8,128)}, f32[1,4096]{1,0:T(1,128)}, f32[8,4096]{1,0:T(8,128)}, f32[8,128]{1,0:T(8,128)}) custom-call(bf16[2432,256]{1,0:T(8,128)(2,1)} %get-tuple-element.17.comp, f32[2176,128]{1,0:T(8,128)} %get-tuple-element.18.shift, f32[2176,128]{1,0:T(8,128)} %get-tuple-element.19.slope, bf16[2176,128]{1,0:T(8,128)(2,1)} %get-tuple-element.20.expo, ...), custom_call_target="tpu_custom_call" | custom-call | tf_op jit(solution)/shard_map/main/pallas_call | solution.py:489
  131.5 1.3 slice_reduce_fusion
  132.8 1.9 %copy.16 = f32[4096,32]{0,1:T(8,128)} copy(f32[4096,32]{0,1:T(8,128)} %bitcast.12) | data formatting | bytes 1048576
  134.7 1.3 copy.17
  136.0 1.6 %copy.18 = f32[4096,8]{0,1:T(8,128)} copy(f32[4096,8]{0,1:T(8,128)} %bitcast.13) | data formatting | bytes 262144
  (2 shorter events, 0.0 us)

commit v4 on v3

--- a/solution.py
+++ b/solution.py
@@ -39,101 +39,6 @@
     return out
 
 
-def exchange_kernel(tiles, small, got, got_small, sends, recvs, sends_s, recvs_s, sends_b, recvs_b, own):
-    me = lax.axis_index("cp")
-    sc = lax.axis_index("sc")
-    core = sc % 2
-    sibling = sc + 1 - 2 * core
-    barrier = pltpu.get_barrier_semaphore()
-
-    def greet(k, _):
-        pl.semaphore_signal(barrier, inc=1, device_id=((me + k) % NCP, sc), device_id_type=MESH)
-        return 0
-
-    lax.fori_loop(1, NCP, greet, 0)
-    pl.semaphore_signal(barrier, inc=1, device_id=(me, sibling), device_id_type=MESH)
-    pl.semaphore_wait(barrier, NCP)
-
-    half = pl.ds(core * 8, 8)
-
-    def row_copy(k):
-        peer = (me + k) % NCP
-        return pltpu.make_async_remote_copy(
-            src_ref=tiles.at[half, (peer - me + NCP) % NCP],
-            dst_ref=got.at[me, half],
-            send_sem=sends.at[k],
-            recv_sem=recvs.at[k],
-            device_id=(peer, sc),
-            device_id_type=MESH,
-        )
-
-    def small_copy(k):
-        peer = (me + k) % NCP
-        return pltpu.make_async_remote_copy(
-            src_ref=small.at[(peer - me + NCP) % NCP],
-            dst_ref=got_small.at[me],
-            send_sem=sends_s.at[k],
-            recv_sem=recvs_s.at[k],
-            device_id=(peer, sc),
-            device_id_type=MESH,
-        )
-
-    def forward(k):
-        source = (me - k + NCP) % NCP
-        return pltpu.make_async_remote_copy(
-            src_ref=got.at[source, half],
-            dst_ref=got.at[source, half],
-            send_sem=sends_b.at[k],
-            recv_sem=recvs_b.at[k],
-            device_id=(me, sibling),
-            device_id_type=MESH,
-        )
-
-    def start(k, _):
-        row_copy(k).start()
-        small_copy(k).start()
-        return 0
-
-    lax.fori_loop(1, NCP, start, 0)
-    mine = pltpu.make_async_copy(tiles.at[:, 0], got.at[me], own.at[0])
-    mine.start()
-    mine_small = pltpu.make_async_copy(small.at[0], got_small.at[me], own.at[1])
-    mine_small.start()
-
-    def pass_on(k, _):
-        row_copy(k).wait_recv()
-        forward(k).start()
-        return 0
-
-    lax.fori_loop(1, NCP, pass_on, 0)
-    mine.wait()
-    mine_small.wait()
-
-    def finish(k, _):
-        row_copy(k).wait_send()
-        small_copy(k).wait()
-        forward(k).wait()
-        return 0
-
-    lax.fori_loop(1, NCP, finish, 0)
-
-
-def exchange(tiles, small):
-    any_spec = pl.BlockSpec(memory_space=pl.ANY)
-    return pl.pallas_call(
-        exchange_kernel,
-        out_shape=(
-            jax.ShapeDtypeStruct((NCP, 16, 16, F), BF),
-            jax.ShapeDtypeStruct((NCP, 16, SEG), BF),
-        ),
-        in_specs=[any_spec] * 2,
-        out_specs=[any_spec] * 2,
-        scratch_shapes=[pltpu.SemaphoreType.DMA((NCP,))] * 6 + [pltpu.SemaphoreType.DMA((2,))],
-        compiler_params=pltpu.CompilerParams(collective_id=0, has_side_effects=True),
-        name="exchange",
-    )(tiles, small)
-
-
 def double_cdf(u):
     far = TAIL[3]
     for coef in TAIL[2::-1]:
@@ -149,60 +54,14 @@
     lax.fori_loop(first, last, body, 0)
 
 
-def compact_kernel(lengths, got, got_small, comp, shift, slope, expo, expo_t, wide):
-    comp[...] = jnp.zeros_like(comp)
-    wide[...] = jnp.zeros_like(wide)
-    index = lax.broadcasted_iota(jnp.int32, (SEG, 128), 0)
-    lane = lax.broadcasted_iota(jnp.int32, (SEG, 128), 1)
-    for block, (start, offset, live) in enumerate(spots(lengths, lax.axis_index("cp"))):
-        at = pl.ds(pl.multiple_of(start * 16, 16), SEG)
-        comp[at, :] = got[block]
-        part = got_small[block].astype(F32)
-        part = jnp.concatenate([part, jnp.zeros((112, SEG), F32)], axis=0).T
-        row = (offset + 16 * (index // 16)) * 16 + index % 16
-        keep = (row < live) | (lane >= 8)
-        wide[at, :] = jnp.where(keep, part, 0.0)
-
-    def scale(i, _):
-        at = pl.ds(pl.multiple_of(i * 128, 128), 128)
-        rows = comp[at, :].astype(F32)
-        total = jnp.sum(rows * rows, axis=1, keepdims=True)
-        by = lax.rsqrt(1.0 + total) * ROOT_HALF
-        slope[at, :] = jnp.broadcast_to(by, (128, 128))
-        part = wide[at, :]
-        shift[at, :] = jnp.broadcast_to(part[:, 8:9] * by, (128, 128))
-        expo[at, :] = part.astype(BF)
-        expo_t[:, at] = part.T[0:16, :].astype(BF)
-        return 0
-
-    lax.fori_loop(0, CAP // 128, scale, 0)
-
-
-def compact(lengths, got, got_small):
-    vmem = pl.BlockSpec(memory_space=pltpu.VMEM)
-    return pl.pallas_call(
-        compact_kernel,
-        out_shape=(
-            jax.ShapeDtypeStruct((CAP + SEG, F), BF),
-            jax.ShapeDtypeStruct((CAP, 128), F32),
-            jax.ShapeDtypeStruct((CAP, 128), F32),
-            jax.ShapeDtypeStruct((CAP, 128), BF),
-            jax.ShapeDtypeStruct((16, CAP), BF),
-        ),
-        in_specs=[pl.BlockSpec(memory_space=pltpu.SMEM), vmem, vmem],
-        out_specs=[vmem] * 5,
-        scratch_shapes=[pltpu.VMEM((CAP + SEG, 128), F32)],
-        name="compact",
-    )(lengths, got, got_small)
-
-
 def main_kernel(
-    comp, shift, slope, expo, expo_t, factors, aversion, lengths, load_out, thr_out, expo_out, risk,
-    full, pack, back, prob, loss, parts, mine, every, stats, weights, turned,
+    tiles, expo_in, thr_in, factors, aversion, lengths, load_out, thr_out, expo_out, risk,
+    got, small, got_small, wide, comp, shift, slope, expo, expo_t, table, lives, full, pack, back, prob, loss, parts, mine, every, stats, weights, turned,
     expo_acc, dates, dates_in, date_sum, date_all,
     load_acc, lat_acc, thr_acc, grads, pair, sum_l, near_l, thr_line, thr_pair, thr_sum, thr_near,
     sends, recvs, sends_g, recvs_g, sends_z, recvs_z, sends_d, recvs_d, sends_e, recvs_e,
     sends_a, recvs_a, sends_b, recvs_b, sends_t, recvs_t, sends_c, recvs_c,
+    sends_x, recvs_x, sends_s, recvs_s, sends_y, recvs_y, own,
 ):
     me = lax.axis_index("cp")
     sc = lax.axis_index("sc")
@@ -219,6 +78,95 @@
             src_ref=src, dst_ref=dst, send_sem=send, recv_sem=recv, device_id=to, device_id_type=MESH
         )
 
+    half = core * 8
+
+    def row_copy(k):
+        peer = (me + k) % NCP
+        return remote(
+            tiles.at[pl.ds(half, 8), (peer - me + NCP) % NCP], got.at[pl.ds(me * 16 + half, 8)],
+            sends_x.at[k], recvs_x.at[k], (peer, sc),
+        )
+
+    def small_copy(k):
+        peer = (me + k) % NCP
+        return remote(
+            small.at[(peer - me + NCP) % NCP], got_small.at[me], sends_s.at[k], recvs_s.at[k], (peer, sc)
+        )
+
+    def pass_on(k):
+        at = pl.ds(((me - k + NCP) % NCP) * 16 + half, 8)
+        return remote(got.at[at], got.at[at], sends_y.at[k], recvs_y.at[k], (me, sibling))
+
+    chunk_of = lax.broadcasted_iota(jnp.int32, (16, 128), 1) // 16
+    limits = jnp.broadcast_to(thr_in[...].astype(F32), (8, ROWS))
+    raw = jnp.concatenate([expo_in[...].astype(F32), limits], axis=0)
+    for t in range(NCP):
+        for h in range(2):
+            mixed = None
+            for q in range(8):
+                tile = 2 * (8 * h + q) + t // 8
+                moved = pltpu.roll(raw[:, 128 * tile : 128 * (tile + 1)], (16 * (q - t % 8)) % 128, 1)
+                mixed = moved if mixed is None else jnp.where(chunk_of == q, moved, mixed)
+            small[t, :, 128 * h : 128 * (h + 1)] = mixed.astype(BF)
+
+    pl.semaphore_wait(barrier, NCP + NSC - 2)
+    run(1, NCP, lambda k: (row_copy(k).start(), small_copy(k).start()))
+    mine_rows = pltpu.make_async_copy(tiles.at[:, 0], got.at[pl.ds(me * 16, 16)], own.at[0])
+    mine_rows.start()
+    got_small[me] = small[0]
+
+    places = spots(lengths, me)
+
+    def tabulate(k):
+        block = jnp.int32(0)
+        begin = jnp.int32(0)
+        offset = places[0][1]
+        live = places[0][2]
+        for i in range(1, NCP):
+            later = k >= places[i][0]
+            block = jnp.where(later, i, block)
+            begin = jnp.where(later, places[i][0], begin)
+            offset = jnp.where(later, places[i][1], offset)
+            live = jnp.where(later, places[i][2], live)
+        slot = jnp.minimum(k - begin, 15)
+        table[k] = block * 16 + slot
+        lives[k] = live - (offset + 16 * slot) * 16 - 32768 * jnp.where(k - begin > 15, 1, 0)
+
+    run(0, CAP // 16, tabulate)
+    run(1, NCP, lambda k: small_copy(k).wait_recv())
+    for block in range(NCP):
+        part = got_small[block].astype(F32)
+        part = jnp.concatenate([part, jnp.zeros((112, SEG), F32)], axis=0).T
+        for slot in range(16):
+            wide[block * 16 + slot] = part[16 * slot : 16 * (slot + 1), :]
+    run(1, NCP, lambda k: (row_copy(k).wait_recv(), pass_on(k).start()))
+    mine_rows.wait()
+    run(1, NCP, lambda k: (row_copy(k).wait_send(), small_copy(k).wait_send(), pass_on(k).wait()))
+
+    row_of = lax.broadcasted_iota(jnp.int32, (16, 128), 0)
+    lane_of = lax.broadcasted_iota(jnp.int32, (16, 128), 1)
+
+    def compact(i):
+        at = pl.ds(pl.multiple_of(i * 128, 128), 128)
+        rows = jnp.concatenate([got[table[8 * i + q]] for q in range(8)], axis=0)
+        part = jnp.concatenate(
+            [
+                jnp.where((row_of < lives[8 * i + q]) | (lane_of >= 8), wide[table[8 * i + q]], 0.0)
+                for q in range(8)
+            ],
+            axis=0,
+        )
+        comp[at, :] = rows
+        rows = rows.astype(F32)
+        total = jnp.sum(rows * rows, axis=1, keepdims=True)
+        by = lax.rsqrt(1.0 + total) * ROOT_HALF
+        slope[at, :] = jnp.broadcast_to(by, (128, 128))
+        shift[at, :] = jnp.broadcast_to(part[:, 8:9] * by, (128, 128))
+        expo[at, :] = part.astype(BF)
+        expo_t[:, at] = part.T[0:16, :].astype(BF)
+
+    run(0, CAP // 128, compact)
+
     def latent(first, count, cols):
         rows = pl.ds(first, count)
         project = lax.dot_general(
@@ -235,7 +183,6 @@
         loss[:, cols] = jnp.dot(expo_t[...], prob[:, cols], preferred_element_type=F32)[0:8, :]
 
     run(0, S // ST, ahead)
-    pl.semaphore_wait(barrier, NCP + NSC - 2)
 
     def part_of(position):
         return pl.ds(pl.multiple_of(position * width, width), width)
@@ -440,7 +387,7 @@
     run(1, NSC, lambda k: (date_out(k).wait_send(), date_share(k).wait_send()))
     near_up(last)
     lane = lax.broadcasted_iota(jnp.int32, (48, SEG), 1)
-    for block, (start, offset, live) in enumerate(spots(lengths, me)):
+    for block, (start, offset, live) in enumerate(places):
         tile = start >> 3
         piece = jnp.concatenate([full[tile], full[tile + 1], full[tile + 2]], axis=1)
         part = jnp.full((48, 384), start & 7, jnp.int32)
@@ -481,7 +428,7 @@
     run(1, NCP, lambda k: back_copy(k).wait_send())
 
 
-def main(comp, shift, slope, expo, expo_t, factors, aversion, lengths):
+def main(tiles, expo_in, thr_in, factors, aversion, lengths):
     vmem = pl.BlockSpec(memory_space=pltpu.VMEM)
     dma = pltpu.SemaphoreType.DMA
     parts = len(CHUNKS)
@@ -494,9 +441,20 @@
             jax.ShapeDtypeStruct((NSC, ROWS), F32),
             jax.ShapeDtypeStruct((8, 128), F32),
         ),
-        in_specs=[vmem] * 6 + [pl.BlockSpec(memory_space=pltpu.SMEM)] * 2,
+        in_specs=[pl.BlockSpec(memory_space=pl.ANY)] + [vmem] * 3 + [pl.BlockSpec(memory_space=pltpu.SMEM)] * 2,
         out_specs=[vmem] * 4,
         scratch_shapes=[
+            pltpu.VMEM((NCP * 16, 16, F), BF),
+            pltpu.VMEM((NCP, 16, SEG), BF),
+            pltpu.VMEM((NCP, 16, SEG), BF),
+            pltpu.VMEM((NCP * 16, 16, 128), F32),
+            pltpu.VMEM((CAP, F), BF),
+            pltpu.VMEM((CAP, 128), F32),
+            pltpu.VMEM((CAP, 128), F32),
+            pltpu.VMEM((CAP, 128), BF),
+            pltpu.VMEM((16, CAP), BF),
+            pltpu.SMEM((CAP // 16,), jnp.int32),
+            pltpu.SMEM((CAP // 16,), jnp.int32),
             pltpu.VMEM((CAP // 128 + 3, 48, 128), F32),
             pltpu.VMEM((NCP, 48, SEG), BF),
             pltpu.VMEM((NCP, 48, SEG), BF),
@@ -542,23 +500,26 @@
             dma((parts, 4)),
             dma((NCP,)),
             dma((NCP,)),
+            dma((NCP,)),
+            dma((NCP,)),
+            dma((NCP,)),
+            dma((NCP,)),
+            dma((NCP,)),
+            dma((NCP,)),
+            dma((1,)),
         ],
         compiler_params=pltpu.CompilerParams(
-            collective_id=1, has_side_effects=True, vmem_limit_bytes=58 * 2**20
+            collective_id=0, has_side_effects=True, vmem_limit_bytes=58 * 2**20
         ),
         name="main",
-    )(comp, shift, slope, expo, expo_t, factors, aversion, lengths)
+    )(tiles, expo_in, thr_in, factors, aversion, lengths)
 
 
 def per_device(factors, loadings, thresholds, exposures, aversion, lengths):
     tiles = loadings.reshape(16, NCP, 16, F)
-    small = jnp.concatenate(
-        [exposures.T, thresholds[None, :], jnp.zeros((7, ROWS), BF)], axis=0
+    load, thr, dates, risk = main(
+        tiles, exposures.T, thresholds.reshape(1, ROWS), factors, aversion, lengths
     )
-    small = small.reshape(16, 16, NCP, 16).transpose(2, 0, 1, 3).reshape(NCP, 16, SEG)
-    got, got_small = exchange(tiles, small)
-    rows = compact(lengths, got.reshape(NCP, SEG, F), got_small)
-    load, thr, dates, risk = main(*rows, factors, aversion, lengths)
     return (load.T, thr.reshape(ROWS), dates.T, risk[:, 0])
 
 

time: 138 us -> 132 us (0.957)
  Pallas kernels: 127 us -> 123 us
  local copies, waits for them, and re-layouts: 9.98 us -> 7.38 us
    pallas_call x2 -> x0, Pallas kernels: 30.5 us -> none  [the longest x1 22.4 us: exchange(): pl.pallas_call(exchange_kernel, out_shape=(jax.ShapeDtypeStruct((NCP, 16,...]
    pallas_call x1, Pallas kernels: 96.2 us -> 123 us  [main(): pl.pallas_call(main_kernel, out_shape=(jax.ShapeDtypeStruct((32, ROWS), F...]
    concatenate x5 -> x0, local copies, waits for them, and re-layouts: 2.27 us -> none  [per_device(): jnp.concatenate([exposures.T, thresholds[None, :], jnp.zeros((7, ROWS), B...]
where the time goes in v4:
time: 132 us; the launch traced here: 131 us
  Pallas kernels  123 us (93%)
  local copies, waits for them, and re-layouts  7.38 us (6%)
    pallas_call x1, Pallas kernels, main(): pl.pallas_call(main_kernel, out_shape=(jax.ShapeDtypeStruct((32, ROWS), F...  123 us
    unnamed x3, local copies, waits for them, and re-layouts  4.76 us

profile of v4, /device:TPU:0, one launch (start us, length us, event | category | flops | bytes accessed | tf_op | source)
XLA Modules:
  0.0 131.5 jit_solution(6642171828692181544)
XLA Ops:
  0.6 1.3 reshape.18.thr_in
  1.9 123.5 %main.1 = (f32[32,4096]{1,0:T(8,128)}, f32[1,4096]{1,0:T(1,128)}, f32[8,4096]{1,0:T(8,128)}, f32[8,128]{1,0:T(8,128)}) custom-call(bf16[16,16,16,256]{3,2,1,0:T(8,128)(2,1)} %bitcast.5, bf16[8,4096]{1,0:T(8,128)(2,1)} %bitcast.8, bf16[1,4096]{1,0:T(2,128)(2,1)} %reshape.18.thr_in, bf16[4096,256]{1,0:T(8,128)(2,1)} %factors.1, f32[8]{0:T(128)} %aversion.1, ...), custom_call_target="tpu_custom_call" | custom-call | tf_op jit(solution)/shard_map/main/pallas_call | solution.py:436
  125.4 1.3 slice_reduce_fusion
  126.7 1.9 %copy.13 = f32[4096,32]{0,1:T(8,128)} copy(f32[4096,32]{0,1:T(8,128)} %bitcast.6) | data formatting | bytes 1048576
  128.6 1.3 %copy.14 = f32[4096]{0:T(1024)} copy(f32[4096]{0:T(1024)} %bitcast.9) | data formatting | bytes 32768
  129.9 1.6 %copy.15 = f32[4096,8]{0,1:T(8,128)} copy(f32[4096,8]{0,1:T(8,128)} %bitcast.7) | data formatting | bytes 262144

commit v5 on v4

--- a/solution.py
+++ b/solution.py
@@ -28,15 +28,17 @@
 
 
 def spots(lengths_ref, position):
-    start = jnp.int32(0)
-    out = []
+    low, high = [], []
+    at = jnp.int32(0)
+    beyond = jnp.int32(0)
     for block in range(NCP):
-        live = lengths_ref[block]
-        tiles = (live + 15) >> 4
         offset = (position - block + NCP) % NCP
-        out.append((start, offset, live))
-        start = start + ((tiles - offset + 15) >> 4)
-    return out
+        tiles = (((lengths_ref[block] + 15) >> 4) - offset + 15) >> 4
+        low.append(at)
+        high.append(beyond)
+        at = at + jnp.minimum(tiles, 8)
+        beyond = beyond + jnp.maximum(tiles - 8, 0)
+    return low, [at + place for place in high], at
 
 
 def double_cdf(u):
@@ -56,7 +58,7 @@
 
 def main_kernel(
     tiles, expo_in, thr_in, factors, aversion, lengths, load_out, thr_out, expo_out, risk,
-    got, small, got_small, wide, comp, shift, slope, expo, expo_t, table, lives, full, pack, back, prob, loss, parts, mine, every, stats, weights, turned,
+    got, got_high, small, got_small, wide, comp, shift, slope, expo, expo_t, table, lives, begins, full, pack, back, prob, loss, parts, mine, every, stats, weights, turned,
     expo_acc, dates, dates_in, date_sum, date_all,
     load_acc, lat_acc, thr_acc, grads, pair, sum_l, near_l, thr_line, thr_pair, thr_sum, thr_near,
     sends, recvs, sends_g, recvs_g, sends_z, recvs_z, sends_d, recvs_d, sends_e, recvs_e,
@@ -78,13 +80,14 @@
             src_ref=src, dst_ref=dst, send_sem=send, recv_sem=recv, device_id=to, device_id_type=MESH
         )
 
-    half = core * 8
-
-    def row_copy(k):
+    half = core * 4
+
+    def row_copy(k, high):
         peer = (me + k) % NCP
         return remote(
-            tiles.at[pl.ds(half, 8), (peer - me + NCP) % NCP], got.at[pl.ds(me * 16 + half, 8)],
-            sends_x.at[k], recvs_x.at[k], (peer, sc),
+            tiles.at[pl.ds(8 * high + half, 4), (peer - me + NCP) % NCP],
+            (got, got_high)[high].at[pl.ds(me * 8 + half, 4)],
+            sends_x.at[high, k], recvs_x.at[high, k], (peer, sc),
         )
 
     def small_copy(k):
@@ -93,9 +96,15 @@
             small.at[(peer - me + NCP) % NCP], got_small.at[me], sends_s.at[k], recvs_s.at[k], (peer, sc)
         )
 
-    def pass_on(k):
-        at = pl.ds(((me - k + NCP) % NCP) * 16 + half, 8)
-        return remote(got.at[at], got.at[at], sends_y.at[k], recvs_y.at[k], (me, sibling))
+    def pass_on(k, high):
+        at = pl.ds(((me - k + NCP) % NCP) * 8 + half, 4)
+        part = (got, got_high)[high].at[at]
+        return remote(part, part, sends_y.at[high, k], recvs_y.at[high, k], (me, sibling))
+
+    def own_copy(high):
+        return pltpu.make_async_copy(
+            tiles.at[pl.ds(8 * high, 8), 0], (got, got_high)[high].at[pl.ds(me * 8, 8)], own.at[high]
+        )
 
     chunk_of = lax.broadcasted_iota(jnp.int32, (16, 128), 1) // 16
     limits = jnp.broadcast_to(thr_in[...].astype(F32), (8, ROWS))
@@ -110,27 +119,36 @@
             small[t, :, 128 * h : 128 * (h + 1)] = mixed.astype(BF)
 
     pl.semaphore_wait(barrier, NCP + NSC - 2)
-    run(1, NCP, lambda k: (row_copy(k).start(), small_copy(k).start()))
-    mine_rows = pltpu.make_async_copy(tiles.at[:, 0], got.at[pl.ds(me * 16, 16)], own.at[0])
-    mine_rows.start()
+    run(1, NCP, lambda k: (small_copy(k).start(), row_copy(k, 0).start()))
+    own_copy(0).start()
+    run(1, NCP, lambda k: row_copy(k, 1).start())
+    own_copy(1).start()
     got_small[me] = small[0]
 
-    places = spots(lengths, me)
+    low, high, lows = spots(lengths, me)
+    for block in range(NCP):
+        begins[block] = low[block]
+        begins[NCP + block] = high[block]
 
     def tabulate(k):
-        block = jnp.int32(0)
-        begin = jnp.int32(0)
-        offset = places[0][1]
-        live = places[0][2]
+        block_low = jnp.int32(0)
+        block_high = jnp.int32(0)
         for i in range(1, NCP):
-            later = k >= places[i][0]
-            block = jnp.where(later, i, block)
-            begin = jnp.where(later, places[i][0], begin)
-            offset = jnp.where(later, places[i][1], offset)
-            live = jnp.where(later, places[i][2], live)
-        slot = jnp.minimum(k - begin, 15)
-        table[k] = block * 16 + slot
-        lives[k] = live - (offset + 16 * slot) * 16 - 32768 * jnp.where(k - begin > 15, 1, 0)
+            block_low = block_low + jnp.where(k >= begins[i], 1, 0)
+            block_high = block_high + jnp.where(k >= begins[NCP + i], 1, 0)
+        slot_low = jnp.clip(k - begins[block_low], 0, 7)
+        past = k - begins[NCP + block_high]
+        slot_high = jnp.clip(past, 0, 7)
+        upper = k >= lows
+        block = jnp.where(upper, block_high, block_low)
+        slot = jnp.where(upper, slot_high + 8, slot_low)
+        table[0, k] = block_low * 8 + slot_low
+        table[1, k] = block_high * 8 + slot_high
+        table[2, k] = block * 16 + slot
+        table[3, k] = jnp.where(upper, 1, 0)
+        offset = (me - block + NCP) & 15
+        spare = jnp.where(upper & (past > 7), 32768, 0)
+        lives[k] = lengths[block] - (offset + 16 * slot) * 16 - spare
 
     run(0, CAP // 16, tabulate)
     run(1, NCP, lambda k: small_copy(k).wait_recv())
@@ -139,25 +157,31 @@
         part = jnp.concatenate([part, jnp.zeros((112, SEG), F32)], axis=0).T
         for slot in range(16):
             wide[block * 16 + slot] = part[16 * slot : 16 * (slot + 1), :]
-    run(1, NCP, lambda k: (row_copy(k).wait_recv(), pass_on(k).start()))
-    mine_rows.wait()
-    run(1, NCP, lambda k: (row_copy(k).wait_send(), small_copy(k).wait_send(), pass_on(k).wait()))
+    run(1, NCP, lambda k: (row_copy(k, 0).wait_recv(), pass_on(k, 0).start()))
+    own_copy(0).wait()
+    run(1, NCP, lambda k: pass_on(k, 0).wait_recv())
 
     row_of = lax.broadcasted_iota(jnp.int32, (16, 128), 0)
     lane_of = lax.broadcasted_iota(jnp.int32, (16, 128), 1)
 
-    def compact(i):
+    def compact(i, mixed):
         at = pl.ds(pl.multiple_of(i * 128, 128), 128)
-        rows = jnp.concatenate([got[table[8 * i + q]] for q in range(8)], axis=0)
+        pieces = []
+        for q in range(8):
+            piece = got[table[0, 8 * i + q]].astype(F32)
+            if mixed:
+                upper = jnp.full((16, F), table[3, 8 * i + q], jnp.int32) > 0
+                piece = jnp.where(upper, got_high[table[1, 8 * i + q]].astype(F32), piece)
+            pieces.append(piece)
+        rows = jnp.concatenate(pieces, axis=0)
         part = jnp.concatenate(
             [
-                jnp.where((row_of < lives[8 * i + q]) | (lane_of >= 8), wide[table[8 * i + q]], 0.0)
+                jnp.where((row_of < lives[8 * i + q]) | (lane_of >= 8), wide[table[2, 8 * i + q]], 0.0)
                 for q in range(8)
             ],
             axis=0,
         )
-        comp[at, :] = rows
-        rows = rows.astype(F32)
+        comp[at, :] = rows.astype(BF)
         total = jnp.sum(rows * rows, axis=1, keepdims=True)
         by = lax.rsqrt(1.0 + total) * ROOT_HALF
         slope[at, :] = jnp.broadcast_to(by, (128, 128))
@@ -165,8 +189,6 @@
         expo[at, :] = part.astype(BF)
         expo_t[:, at] = part.T[0:16, :].astype(BF)
 
-    run(0, CAP // 128, compact)
-
     def latent(first, count, cols):
         rows = pl.ds(first, count)
         project = lax.dot_general(
@@ -176,13 +198,33 @@
         b = jnp.concatenate([slope[rows, :]] * (ST // 128), axis=1)
         return a - project * b
 
-    def ahead(step):
+    def ahead(step, parts_of):
         cols = pl.ds(pl.multiple_of(step * ST, ST), ST)
-        for first, count in CHUNKS:
+        for first, count in parts_of:
             prob[pl.ds(first, count), cols] = double_cdf(latent(first, count, cols)).astype(BF)
+
+    def ahead_pass(step):
+        ahead(step, CHUNKS[:1])
+        for j in range(3):
+            k = 1 + (step - 2) * 3 + j
+            row_copy(k, 1).wait_recv()
+            pass_on(k, 1).start()
+
+    def ahead_rest(step):
+        cols = pl.ds(pl.multiple_of(step * ST, ST), ST)
+        ahead(step, CHUNKS[1:])
         loss[:, cols] = jnp.dot(expo_t[...], prob[:, cols], preferred_element_type=F32)[0:8, :]
 
-    run(0, S // ST, ahead)
+    run(0, CHUNKS[0][1] // 128, lambda i: compact(i, False))
+    run(0, 2, lambda step: ahead(step, CHUNKS[:1]))
+    run(2, 7, ahead_pass)
+    run(7, S // ST, lambda step: ahead(step, CHUNKS[:1]))
+    own_copy(1).wait()
+    run(1, NCP, lambda k: pass_on(k, 1).wait_recv())
+    run(CHUNKS[0][1] // 128, CAP // 128, lambda i: compact(i, True))
+    run(0, S // ST, ahead_rest)
+    run(1, NCP, lambda k: (row_copy(k, 0).wait_send(), row_copy(k, 1).wait_send(), small_copy(k).wait_send()))
+    run(1, NCP, lambda k: (pass_on(k, 0).wait_send(), pass_on(k, 1).wait_send()))
 
     def part_of(position):
         return pl.ds(pl.multiple_of(position * width, width), width)
@@ -386,15 +428,19 @@
     pair_up(last)
     run(1, NSC, lambda k: (date_out(k).wait_send(), date_share(k).wait_send()))
     near_up(last)
-    lane = lax.broadcasted_iota(jnp.int32, (48, SEG), 1)
-    for block, (start, offset, live) in enumerate(places):
-        tile = start >> 3
-        piece = jnp.concatenate([full[tile], full[tile + 1], full[tile + 2]], axis=1)
-        part = jnp.full((48, 384), start & 7, jnp.int32)
-        for bit in (1, 2, 4):
-            piece = jnp.where(part & bit != 0, pltpu.roll(piece, 384 - 16 * bit, 1), piece)
-        row = (offset + 16 * (lane // 16)) * 16 + lane % 16
-        pack[block] = jnp.where(row < live, piece[:, 0:SEG], 0.0).astype(BF)
+    lane = lax.broadcasted_iota(jnp.int32, (48, 128), 1)
+    for block in range(NCP):
+        offset = (me - block + NCP) % NCP
+        for upper, start in ((0, low[block]), (1, high[block])):
+            tile = start >> 3
+            piece = jnp.concatenate([full[tile], full[tile + 1]], axis=1)
+            part = jnp.full((48, 256), start & 7, jnp.int32)
+            for bit in (1, 2, 4):
+                piece = jnp.where(part & bit != 0, pltpu.roll(piece, 256 - 16 * bit, 1), piece)
+            row = (offset + 16 * (8 * upper + lane // 16)) * 16 + lane % 16
+            pack[block, :, 128 * upper : 128 * (upper + 1)] = jnp.where(
+                row < lengths[block], piece[:, 0:128], 0.0
+            ).astype(BF)
 
     def back_copy(k):
         peer = (me + k) % NCP
@@ -444,7 +490,8 @@
         in_specs=[pl.BlockSpec(memory_space=pl.ANY)] + [vmem] * 3 + [pl.BlockSpec(memory_space=pltpu.SMEM)] * 2,
         out_specs=[vmem] * 4,
         scratch_shapes=[
-            pltpu.VMEM((NCP * 16, 16, F), BF),
+            pltpu.VMEM((NCP * 8, 16, F), BF),
+            pltpu.VMEM((NCP * 8, 16, F), BF),
             pltpu.VMEM((NCP, 16, SEG), BF),
             pltpu.VMEM((NCP, 16, SEG), BF),
             pltpu.VMEM((NCP * 16, 16, 128), F32),
@@ -453,8 +500,9 @@
             pltpu.VMEM((CAP, 128), F32),
             pltpu.VMEM((CAP, 128), BF),
             pltpu.VMEM((16, CAP), BF),
+            pltpu.SMEM((4, CAP // 16), jnp.int32),
             pltpu.SMEM((CAP // 16,), jnp.int32),
-            pltpu.SMEM((CAP // 16,), jnp.int32),
+            pltpu.SMEM((2 * NCP,), jnp.int32),
             pltpu.VMEM((CAP // 128 + 3, 48, 128), F32),
             pltpu.VMEM((NCP, 48, SEG), BF),
             pltpu.VMEM((NCP, 48, SEG), BF),
@@ -500,13 +548,13 @@
             dma((parts, 4)),
             dma((NCP,)),
             dma((NCP,)),
-            dma((NCP,)),
-            dma((NCP,)),
-            dma((NCP,)),
-            dma((NCP,)),
-            dma((NCP,)),
-            dma((NCP,)),
-            dma((1,)),
+            dma((2, NCP)),
+            dma((2, NCP)),
+            dma((NCP,)),
+            dma((NCP,)),
+            dma((2, NCP)),
+            dma((2, NCP)),
+            dma((2,)),
         ],
         compiler_params=pltpu.CompilerParams(
             collective_id=0, has_side_effects=True, vmem_limit_bytes=58 * 2**20

time: 132 us -> 129 us (0.977)
  Pallas kernels: 123 us -> 120 us
    pallas_call x1, Pallas kernels: 123 us -> 120 us  [main(): pl.pallas_call(main_kernel, out_shape=(jax.ShapeDtypeStruct((32, ROWS), F...]
where the time goes in v5:
time: 129 us; the launch traced here: 128 us
  Pallas kernels  120 us (93%)
  local copies, waits for them, and re-layouts  7.38 us (6%)
    pallas_call x1, Pallas kernels, main(): pl.pallas_call(main_kernel, out_shape=(jax.ShapeDtypeStruct((32, ROWS), F...  120 us
    unnamed x3, local copies, waits for them, and re-layouts  4.76 us

profile of v5, /device:TPU:0, one launch (start us, length us, event | category | flops | bytes accessed | tf_op | source)
XLA Modules:
  0.0 128.2 jit_solution(2256378979169209182)
XLA Ops:
  0.6 1.3 %reshape.18.thr_in = bf16[1,4096]{1,0:T(2,128)(2,1)} reshape(bf16[4096]{0:T(1024)(128)(2,1)} %param.8) | data formatting | bytes 16384 | tf_op jit(solution)/shard_map/reshape | solution.py:569
  1.9 120.2 %main.1 = (f32[32,4096]{1,0:T(8,128)}, f32[1,4096]{1,0:T(1,128)}, f32[8,4096]{1,0:T(8,128)}, f32[8,128]{1,0:T(8,128)}) custom-call(bf16[16,16,16,256]{3,2,1,0:T(8,128)(2,1)} %bitcast.5, bf16[8,4096]{1,0:T(8,128)(2,1)} %bitcast.8, bf16[1,4096]{1,0:T(2,128)(2,1)} %reshape.18.thr_in, bf16[4096,256]{1,0:T(8,128)(2,1)} %factors.1, f32[8]{0:T(128)} %aversion.1, ...), custom_call_target="tpu_custom_call" | custom-call | tf_op jit(solution)/shard_map/main/pallas_call | solution.py:482
  122.1 1.3 %slice_reduce_fusion = f32[8]{0:T(128)} fusion(f32[8,128]{1,0:T(8,128)} %get-tuple-element.11), kind=kLoop, calls=%fused_computation | loop fusion | bytes 64 | tf_op jit(solution)/shard_map/slice | solution.py:571
  123.4 1.9 %copy.13 = f32[4096,32]{0,1:T(8,128)} copy(f32[4096,32]{0,1:T(8,128)} %bitcast.6) | data formatting | bytes 1048576
  125.3 1.3 %copy.14 = f32[4096]{0:T(1024)} copy(f32[4096]{0:T(1024)} %bitcast.9) | data formatting | bytes 32768
  126.6 1.6 %copy.15 = f32[4096,8]{0,1:T(8,128)} copy(f32[4096,8]{0,1:T(8,128)} %bitcast.7) | data formatting | bytes 262144

commit v6 on v5

--- a/solution.py
+++ b/solution.py
@@ -18,11 +18,12 @@
 LIVE = 32768
 SCEN = 32768
 ST = 512
-CHUNKS = ((0, 768), (768, 768), (1536, 640))
+CHUNKS = ((0, 896), (896, 768), (1664, 512))
 ROOT_HALF = 0.7071067811865476
 LOG2E = 1.4426950408889634
 FAR = -3.1
 TAIL = (-0.750217616, 0.756257034, -1.37553279, 0.0025935648)
+KEPT = 1
 BF = jnp.bfloat16
 F32 = jnp.float32
 
@@ -58,7 +59,7 @@
 
 def main_kernel(
     tiles, expo_in, thr_in, factors, aversion, lengths, load_out, thr_out, expo_out, risk,
-    got, got_high, small, got_small, wide, comp, shift, slope, expo, expo_t, table, lives, begins, full, pack, back, prob, loss, parts, mine, every, stats, weights, turned,
+    got, got_high, small, got_small, wide, comp, shift, slope, expo, expo_t, table, lives, begins, kept, full, pack, back, prob, loss, parts, mine, every, stats, weights, turned,
     expo_acc, dates, dates_in, date_sum, date_all,
     load_acc, lat_acc, thr_acc, grads, pair, sum_l, near_l, thr_line, thr_pair, thr_sum, thr_near,
     sends, recvs, sends_g, recvs_g, sends_z, recvs_z, sends_d, recvs_d, sends_e, recvs_e,
@@ -201,7 +202,10 @@
     def ahead(step, parts_of):
         cols = pl.ds(pl.multiple_of(step * ST, ST), ST)
         for first, count in parts_of:
-            prob[pl.ds(first, count), cols] = double_cdf(latent(first, count, cols)).astype(BF)
+            u = latent(first, count, cols)
+            if (first, count) == CHUNKS[KEPT]:
+                kept[:, cols] = u
+            prob[pl.ds(first, count), cols] = double_cdf(u).astype(BF)
 
     def ahead_pass(step):
         ahead(step, CHUNKS[:1])
@@ -335,7 +339,7 @@
         def step(i):
             cols = pl.ds(pl.multiple_of(i * ST, ST), ST)
             pull = jnp.dot(expo[rows, 0:16], weights[:, cols], preferred_element_type=F32)
-            u = latent(first, count, cols)
+            u = kept[:, cols] if c == KEPT else latent(first, count, cols)
             heavy = pull * jnp.exp2(u * u * (-LOG2E))
             lat = heavy * u
             lat_sum = lat[:, 0:128]
@@ -358,12 +362,12 @@
             acc = pl.ds(pl.multiple_of(i * 128, 128), 128)
             by = slope[rows, 0:1] * math.sqrt(2.0)
             lat = jnp.sum(lat_acc[acc, :], axis=1, keepdims=True) * (scale * math.sqrt(2.0))
-            thr = jnp.sum(thr_acc[acc, :], axis=1, keepdims=True) * scale * by
+            thr = jnp.sum((thr_acc[acc, :] * (scale * by)).T, axis=0, keepdims=True)
             grad = -(load_acc[acc, :] * (scale * by)) - (lat * by * by) * comp[rows, :].astype(F32)
             flat = grad.T
             for j in range(NSC):
                 grads[j, :, rows] = flat[32 * j : 32 * (j + 1), :]
-            thr_line[:, rows] = jnp.broadcast_to(thr, (128, 128)).T[0:1, :]
+            thr_line[:, rows] = thr
 
         run(0, count // 128, one)
         for k in (2, 1, 3, 0):
@@ -503,6 +507,7 @@
             pltpu.SMEM((4, CAP // 16), jnp.int32),
             pltpu.SMEM((CAP // 16,), jnp.int32),
             pltpu.SMEM((2 * NCP,), jnp.int32),
+            pltpu.VMEM((CHUNKS[KEPT][1], S), F32),
             pltpu.VMEM((CAP // 128 + 3, 48, 128), F32),
             pltpu.VMEM((NCP, 48, SEG), BF),
             pltpu.VMEM((NCP, 48, SEG), BF),
@@ -557,7 +562,7 @@
             dma((2,)),
         ],
         compiler_params=pltpu.CompilerParams(
-            collective_id=0, has_side_effects=True, vmem_limit_bytes=58 * 2**20
+            collective_id=0, has_side_effects=True, vmem_limit_bytes=60 * 2**20
         ),
         name="main",
     )(tiles, expo_in, thr_in, factors, aversion, lengths)

time: 129 us -> 128 us (level)
  no operation moved by 1% of the time
where the time goes in v6:
time: 128 us; the launch traced here: 127 us
  Pallas kernels  119 us (93%)
  local copies, waits for them, and re-layouts  7.38 us (6%)
    pallas_call x1, Pallas kernels, main(): pl.pallas_call(main_kernel, out_shape=(jax.ShapeDtypeStruct((32, ROWS), F...  119 us
    unnamed x3, local copies, waits for them, and re-layouts  4.76 us

profile of v6, /device:TPU:0, one launch (start us, length us, event | category | flops | bytes accessed | tf_op | source)
XLA Modules:
  0.0 127.3 jit_solution(17270318976409899475)
XLA Ops:
  0.6 1.3 %reshape.18.thr_in = bf16[1,4096]{1,0:T(2,128)(2,1)} reshape(bf16[4096]{0:T(1024)(128)(2,1)} %param.8) | data formatting | bytes 16384 | tf_op jit(solution)/shard_map/reshape | solution.py:574
  1.9 119.3 %main.1 = (f32[32,4096]{1,0:T(8,128)}, f32[1,4096]{1,0:T(1,128)}, f32[8,4096]{1,0:T(8,128)}, f32[8,128]{1,0:T(8,128)}) custom-call(bf16[16,16,16,256]{3,2,1,0:T(8,128)(2,1)} %bitcast.5, bf16[8,4096]{1,0:T(8,128)(2,1)} %bitcast.8, bf16[1,4096]{1,0:T(2,128)(2,1)} %reshape.18.thr_in, bf16[4096,256]{1,0:T(8,128)(2,1)} %factors.1, f32[8]{0:T(128)} %aversion.1, ...), custom_call_target="tpu_custom_call" | custom-call | tf_op jit(solution)/shard_map/main/pallas_call | solution.py:486
  121.2 1.3 %slice_reduce_fusion = f32[8]{0:T(128)} fusion(f32[8,128]{1,0:T(8,128)} %get-tuple-element.11), kind=kLoop, calls=%fused_computation | loop fusion | bytes 64 | tf_op jit(solution)/shard_map/slice | solution.py:576
  122.6 1.9 %copy.13 = f32[4096,32]{0,1:T(8,128)} copy(f32[4096,32]{0,1:T(8,128)} %bitcast.6) | data formatting | bytes 1048576
  124.4 1.3 %copy.14 = f32[4096]{0:T(1024)} copy(f32[4096]{0:T(1024)} %bitcast.9) | data formatting | bytes 32768
  125.7 1.6 %copy.15 = f32[4096,8]{0,1:T(8,128)} copy(f32[4096,8]{0,1:T(8,128)} %bitcast.7) | data formatting | bytes 262144

commit v7 on v6

--- a/solution.py
+++ b/solution.py
@@ -108,7 +108,7 @@
         )
 
     chunk_of = lax.broadcasted_iota(jnp.int32, (16, 128), 1) // 16
-    limits = jnp.broadcast_to(thr_in[...].astype(F32), (8, ROWS))
+    limits = jnp.broadcast_to(thr_in[...].astype(F32).reshape(1, ROWS), (8, ROWS))
     raw = jnp.concatenate([expo_in[...].astype(F32), limits], axis=0)
     for t in range(NCP):
         for h in range(2):
@@ -571,7 +571,7 @@
 def per_device(factors, loadings, thresholds, exposures, aversion, lengths):
     tiles = loadings.reshape(16, NCP, 16, F)
     load, thr, dates, risk = main(
-        tiles, exposures.T, thresholds.reshape(1, ROWS), factors, aversion, lengths
+        tiles, exposures.T, thresholds, factors, aversion, lengths
     )
     return (load.T, thr.reshape(ROWS), dates.T, risk[:, 0])
 

time: 128 us -> 127 us (level)
  local copies, waits for them, and re-layouts: 7.38 us -> 6.07 us
    reshape x1 -> x0, local copies, waits for them, and re-layouts: 1.31 us -> none  [per_device(): thresholds.reshape(1, ROWS)]
where the time goes in v7:
time: 127 us; the launch traced here: 126 us
  Pallas kernels  119 us (94%)
  local copies, waits for them, and re-layouts  6.07 us (5%)
    pallas_call x1, Pallas kernels, main(): pl.pallas_call(main_kernel, out_shape=(jax.ShapeDtypeStruct((32, ROWS), F...  119 us
    unnamed x3, local copies, waits for them, and re-layouts  4.76 us

profile of v7, /device:TPU:0, one launch (start us, length us, event | category | flops | bytes accessed | tf_op | source)
XLA Modules:
  0.0 126.1 jit_solution(14345096918761772706)
XLA Ops:
  0.6 119.4 %main.1 = (f32[32,4096]{1,0:T(8,128)}, f32[1,4096]{1,0:T(1,128)}, f32[8,4096]{1,0:T(8,128)}, f32[8,128]{1,0:T(8,128)}) custom-call(bf16[16,16,16,256]{3,2,1,0:T(8,128)(2,1)} %bitcast.5, bf16[8,4096]{1,0:T(8,128)(2,1)} %bitcast.8, bf16[4096]{0:T(1024)(128)(2,1)} %thr_in.1, bf16[4096,256]{1,0:T(8,128)(2,1)} %factors.1, f32[8]{0:T(128)} %aversion.1, s32[16]{0:T(128)} %lengths.1), custom_call_target="tpu_custom_call" | custom-call | tf_op jit(solution)/shard_map/main/pallas_call | solution.py:486
  120.1 1.3 %slice_reduce_fusion = f32[8]{0:T(128)} fusion(f32[8,128]{1,0:T(8,128)} %get-tuple-element.11), kind=kLoop, calls=%fused_computation | loop fusion | bytes 64 | tf_op jit(solution)/shard_map/slice | solution.py:576
  121.4 1.9 %copy.13 = f32[4096,32]{0,1:T(8,128)} copy(f32[4096,32]{0,1:T(8,128)} %bitcast.6) | data formatting | bytes 1048576
  123.2 1.3 %copy.14 = f32[4096]{0:T(1024)} copy(f32[4096]{0:T(1024)} %bitcast.9) | data formatting | bytes 32768
  124.6 1.6 %copy.15 = f32[4096,8]{0,1:T(8,128)} copy(f32[4096,8]{0,1:T(8,128)} %bitcast.7) | data formatting | bytes 262144
